TPU v7x, 256 devices: a whole 4x4x8 slice. The times are simulated.
256 devices in a mesh: row: 16 (over y_lo, z), col: 16 (over x, y_hi, core).
Axes of the slice: x: 4, y: 4 (y_hi: 2, y_lo: 2; y = y_hi * 2 + y_lo), z: 8, core: 2. Of those that a mesh axis runs over, the one named last changes fastest.
Arguments:
- features: bfloat16 [16, 16, 32, 1024], P('col', 'row'), may hold values from -6 to 6
- inv_scales: float32 [32], replicated, may hold values from 0.05 to 0.3
- inverse_tiles: bfloat16 [16, 16, 6, 1024, 1024], P('row', 'col'), may hold values from -6 to 6
- tile_list: int32 [16, 16, 6, 2], P('row', 'col'), may hold values from 0 to 255, as said below
- live_count: int32 [16, 16], P('row', 'col'), may hold values from 1 to 6
Outputs:
- feature_grad: float32 [16, 16, 32, 1024], P('col', 'row')
Inputs may be any that keep to these rules, and one draw needn't show every extreme that they name: `tile_list`: the slot of grid position (r, c) holds a tile (I, J) with I mod 16 == r, J // 16 == c and J <= I; tiles may repeat.
All inputs are finite; a program needn't handle non-finite values.
Results may differ from a plain program's by a relative error of at most 0.0095.
Values may be sent and summed in bfloat16 or wider, within the bound.
No kernel may reach another device: no remote copies, remote signals or barrier semaphores. Data moves between devices by JAX's collectives and lax.ppermute only.
A program may use at most 128 MiB of HBM per device.

v0:
```python
import jax
import jax.numpy as jnp
from jax import lax
from jax.sharding import PartitionSpec as P


def scale_blocks(blocks, inv_scales):
    scaled = (inv_scales[None, :, None] * blocks.astype(jnp.float32)).astype(jnp.bfloat16)
    norms = jnp.sum(jnp.square(scaled.astype(jnp.float32)), axis=1)
    return (scaled, norms)


def body(features, inv_scales, inverse_tiles, tile_list, live_count):
    row_count = lax.axis_size("row")
    row_pos = lax.axis_index("row")
    col_pos = lax.axis_index("col")
    column_set = lax.all_gather(features, "row", axis=1, tiled=True)[0]
    everything = lax.all_gather(column_set[None], "col", axis=0, tiled=True)
    row_set = lax.dynamic_index_in_dim(everything, row_pos, 1, keepdims=False)
    row_scaled, row_norms = scale_blocks(row_set, inv_scales)
    col_scaled, col_norms = scale_blocks(column_set, inv_scales)
    my_tiles = inverse_tiles[0, 0]
    my_list = tile_list[0, 0]
    live = live_count[0, 0]
    root_five = jnp.sqrt(jnp.float32(5.0))

    def one_tile(slot, carry):
        row_acc, col_acc = carry
        ib = my_list[slot, 0]
        jb = my_list[slot, 1]
        row_slot = ib // row_count
        col_slot = jb - col_pos * row_count
        ui = lax.dynamic_index_in_dim(row_scaled, row_slot, 0, keepdims=False)
        uj = lax.dynamic_index_in_dim(col_scaled, col_slot, 0, keepdims=False)
        qi = lax.dynamic_index_in_dim(row_norms, row_slot, 0, keepdims=False)
        qj = lax.dynamic_index_in_dim(col_norms, col_slot, 0, keepdims=False)
        zi = lax.dynamic_index_in_dim(row_set, row_slot, 0, keepdims=False)
        zj = lax.dynamic_index_in_dim(column_set, col_slot, 0, keepdims=False)
        weights = lax.dynamic_index_in_dim(my_tiles, slot, 0, keepdims=False)
        cross = lax.dot_general(
            ui, uj, (((0,), (0,)), ((), ())), preferred_element_type=jnp.float32
        )
        dist = jnp.sqrt(jnp.maximum(qi[:, None] + qj[None, :] - 2.0 * cross, 0.0))
        mult = jnp.where(ib == jb, 1.0, 2.0).astype(jnp.float32)
        coeff = (
            mult
            * weights.astype(jnp.float32)
            * (-5.0 / 3.0)
            * (1.0 + root_five * dist)
            * jnp.exp(-root_five * dist)
        )
        coeff_b = coeff.astype(jnp.bfloat16)
        row_term = zi.astype(jnp.float32) * jnp.sum(coeff, axis=1)[None, :] - lax.dot_general(
            zj, coeff_b, (((1,), (1,)), ((), ())), preferred_element_type=jnp.float32
        )
        col_term = zj.astype(jnp.float32) * jnp.sum(coeff, axis=0)[None, :] - jnp.dot(
            zi, coeff_b, preferred_element_type=jnp.float32
        )
        old_row = lax.dynamic_index_in_dim(row_acc, row_slot, 0, keepdims=True)
        row_acc = lax.dynamic_update_index_in_dim(row_acc, old_row + row_term[None], row_slot, 0)
        old_col = lax.dynamic_index_in_dim(col_acc, col_slot, 0, keepdims=True)
        col_acc = lax.dynamic_update_index_in_dim(col_acc, old_col + col_term[None], col_slot, 0)
        return (row_acc, col_acc)

    row_start = jnp.zeros(row_set.shape, jnp.float32)
    col_start = jnp.zeros(column_set.shape, jnp.float32)
    row_acc, col_acc = lax.fori_loop(0, live, one_tile, (row_start, col_start))
    row_part = lax.psum_scatter(row_acc, "col", scatter_dimension=0, tiled=True)
    col_part = lax.psum_scatter(col_acc, "row", scatter_dimension=0, tiled=True)
    summed = row_part[0] + col_part[0]
    grad = jnp.square(inv_scales)[:, None] * summed
    return grad[None, None]


def solution(mesh):
    return jax.shard_map(
        body,
        mesh=mesh,
        in_specs=(
            P("col", "row", None, None),
            P(),
            P("row", "col", None, None, None),
            P("row", "col", None, None),
            P("row", "col"),
        ),
        out_specs=P("col", "row", None, None),
        check_vma=False,
    )
```

profile of v0, /device:TPU:16, one launch (start us, length us, event | category | flops | bytes accessed | tf_op | source)
XLA Modules:
  0.0 451.3 jit_solution(15535596193825509633)
XLA Ops:
  6.5 0.0 all-gather.3.cloned.1.call-start
  6.5 0.7 all-gather.3.cloned.1.call-update
  7.3 0.0 all-gather.5.cloned.1.call-start
  7.3 73.6 %all-gather.3.cloned.1.call-done = bf16[1,16,32,1024]{3,2,0,1:T(8,128)(2,1)} async-done(((bf16[1,1,32,1024]{3,2,0,1:T(8,128)(2,1)}), bf16[1,16,32,1024]{3,2,0,1:T(8,128)(2,1)}) %all-gather.3.cloned.1.call-update) | async-done | bytes 1048592 | tf_op jit(solution)/shard_map/all_gather | solution.py:17
  80.9 0.0 all-gather.5.cloned.1.call-update
  80.9 0.0 reduce-scatter.3.cloned.1.call-start
  81.0 113.2 %all-gather.5.cloned.1.call-done = bf16[16,16,32,1024]{3,2,1,0:T(8,128)(2,1)} async-done(((bf16[1,16,32,1024]{3,2,1,0:T(8,128)(2,1)}), bf16[16,16,32,1024]{3,2,1,0:T(8,128)(2,1)}) %all-gather.5.cloned.1.call-update) | async-done | bytes 16777232 | tf_op jit(solution)/shard_map/all_gather | solution.py:18
  194.2 3.8 multiply_reduce_fusion
  198.0 0.0 copy-start.1
  198.0 0.2 broadcast.62
  198.3 1.6 broadcast.62.clone
  199.8 0.0 copy-done.1
  199.8 44.3 %while.14 = (s32[]{:T(128)}, f32[16,32,1024]{2,1,0:T(8,128)S(1)}, f32[16,32,1024]{2,1,0:T(8,128)}, s32[]{:T(128)}, s32[6,2]{0,1:T(2,128)S(1)}, /*index=5*/bf16[1...) while((s32[]{:T(128)}, f32[16,32,1024]{2,1,0:T(8,128)S(1)}, ...), condition=%wide.region_5.6_spmd, body=%wide.region_2.5_spmd.sunk | while | flops 217315360 | bytes 9347615 | solution.py:67
  200.5 0.7 constant_dynamic-slice_fusion.6
  205.5 5.2 %fusion.34 = (f32[1024]{0:T(1024)S(1)}, f32[1024]{0:T(1024)S(1)}, bf16[1024,1024]{1,0:T(8,128)(2,1)S(1)}) fusion(bf16[16,32,1024]{2,1,0:T(8,128)(2,1)} %get-tuple-element.368, s32[]{:T(128)S(6)} %select_n.61, bf16[16,32,1024]{2,1,0:T(8,128)(2,1)} %get-tuple-element.367, s32[]{:T(128)S(6)} %select_n.60, f32[1024]{0:T(1024)S(1)} %bitcast.83, ...), kind=kOutput, calls=%fused_computation.33.clone.1 | convolution fusion | flops 82835456 | bytes 4341776 | tf_op jit(solution)/shard_map/while/body/dot_general | solution.py:40
  210.8 2.0 fusion.36
  212.8 1.6 fusion.35
  215.0 0.7 constant_dynamic-slice_fusion.6
  220.0 5.2 %fusion.34 = (f32[1024]{0:T(1024)S(1)}, f32[1024]{0:T(1024)S(1)}, bf16[1024,1024]{1,0:T(8,128)(2,1)S(1)}) fusion(bf16[16,32,1024]{2,1,0:T(8,128)(2,1)} %get-tuple-element.368, s32[]{:T(128)S(6)} %select_n.61, bf16[16,32,1024]{2,1,0:T(8,128)(2,1)} %get-tuple-element.367, s32[]{:T(128)S(6)} %select_n.60, f32[1024]{0:T(1024)S(1)} %bitcast.83, ...), kind=kOutput, calls=%fused_computation.33.clone.1 | convolution fusion | flops 82835456 | bytes 4341776 | tf_op jit(solution)/shard_map/while/body/dot_general | solution.py:40
  225.3 2.1 fusion.36
  227.3 1.6 fusion.35
  229.6 0.7 constant_dynamic-slice_fusion.6
  234.6 5.2 %fusion.34 = (f32[1024]{0:T(1024)S(1)}, f32[1024]{0:T(1024)S(1)}, bf16[1024,1024]{1,0:T(8,128)(2,1)S(1)}) fusion(bf16[16,32,1024]{2,1,0:T(8,128)(2,1)} %get-tuple-element.368, s32[]{:T(128)S(6)} %select_n.61, bf16[16,32,1024]{2,1,0:T(8,128)(2,1)} %get-tuple-element.367, s32[]{:T(128)S(6)} %select_n.60, f32[1024]{0:T(1024)S(1)} %bitcast.83, ...), kind=kOutput, calls=%fused_computation.33.clone.1 | convolution fusion | flops 82835456 | bytes 4341776 | tf_op jit(solution)/shard_map/while/body/dot_general | solution.py:40
  239.8 2.1 fusion.36
  241.9 1.6 fusion.35
  244.1 0.0 copy-start
  244.1 0.0 copy-start.2
  244.1 1.3 copy-done
  245.5 0.0 reduce-scatter.3.cloned.1.call-update
  245.5 0.0 reduce-scatter.5.cloned.1.call-start
  245.5 0.5 reduce-scatter.5.cloned.1.call-update
  246.1 0.0 copy-done.2
  246.1 120.8 %reduce-scatter.3.cloned.1.call-done = f32[1,32,1024]{2,1,0:T(8,128)} async-done(((f32[16,32,1024]{2,1,0:T(8,128)}), f32[1,32,1024]{2,1,0:T(8,128)}) %reduce-scatter.3.cloned.1.call-update) | async-done | bytes 131088 | tf_op jit(solution)/shard_map/reduce_scatter | solution.py:68
  366.8 76.2 %reduce-scatter.5.cloned.1.call-done = f32[1,32,1024]{2,1,0:T(8,128)} async-done(((f32[16,32,1024]{2,1,0:T(8,128)}), f32[1,32,1024]{2,1,0:T(8,128)}) %reduce-scatter.5.cloned.1.call-update) | async-done | bytes 131088 | tf_op jit(solution)/shard_map/reduce_scatter | solution.py:69
  443.0 1.7 bitcast_multiply_fusion.1
  (4 shorter events, 0.1 us)
Async XLA Ops:
  6.5 74.4 %all-gather.3.cloned.1.call-start = ((), (), s32[]{:S(2)}) async-start(), calls=%async_computation.2 | async-start | bytes 1114112 | tf_op jit(solution)/shard_map/all_gather | solution.py:17
  7.3 186.9 %all-gather.5.cloned.1.call-start = ((), (), s32[]{:S(2)}) async-start(), calls=%async_computation.3 | async-start | bytes 17825792 | tf_op jit(solution)/shard_map/all_gather | solution.py:18
  80.9 285.9 %reduce-scatter.3.cloned.1.call-start = ((), (), s32[]{:S(2)}) async-start(), calls=%async_computation.4 | async-start | bytes 2228224 | tf_op jit(solution)/shard_map/reduce_scatter | solution.py:68
  198.0 1.8 copy-start.1
  244.1 1.3 copy-start
  244.1 1.9 copy-start.2
  245.5 197.5 %reduce-scatter.5.cloned.1.call-start = ((), (), s32[]{:S(2)}) async-start(), calls=%async_computation.5 | async-start | bytes 2228224 | tf_op jit(solution)/shard_map/reduce_scatter | solution.py:69
Sparse Core Ops, SparseCore 0:
  9.1 71.7 all-gather.2
  83.6 110.5 all-gather.4
  245.6 121.1 reduce-scatter.2
  369.2 73.7 reduce-scatter.4
where the time goes:
time: 453 us; the launch traced here: 451 us
  waiting for transfers between devices  385 us (85%)
  matrix products  26.6 us (6%)
  loops' own time  15.7 us (3%)
  between operations  13.2 us (3%)
  other arithmetic  5.53 us (1%)
  local copies, waits for them, and re-layouts  5.14 us (1%)
    reduce_scatter x1, waiting for transfers between devices, body(): row_part = lax.psum_scatter(row_acc, 'col', scatter_dimension=0, tiled=True)  121 us
    all_gather x1, waiting for transfers between devices, body(): everything = lax.all_gather(column_set[None], 'col', axis=0, tiled=True)  113 us
    reduce_scatter x1, waiting for transfers between devices, body(): col_part = lax.psum_scatter(col_acc, 'row', scatter_dimension=0, tiled=True)  76.2 us
    all_gather x1, waiting for transfers between devices, body(): column_set = lax.all_gather(features, 'row', axis=1, tiled=True)[0]  73.6 us
    dot_general x3, matrix products, one_tile(): lax.dot_general(ui, uj, (((0,), (0,)), ((), ())), preferred_element_type=...  15.7 us
    another operation x1, loops' own time, body(): row_acc, col_acc = lax.fori_loop(0, live, one_tile, (row_start, col_start))  15.7 us
  transfers between devices with their start and end apart: 4, of which 4 were waited for; matrix products, arithmetic and copies ran while one was open for 0% of the time, Pallas kernels for 0%

commit v1 on v0

v1 whole, which is shorter than its diff:
```python
import jax
import jax.numpy as jnp
from jax import lax
from jax.experimental import pallas as pl
from jax.experimental.pallas import tpu as pltpu
from jax.sharding import PartitionSpec as P

F, TB, S, N = 32, 1024, 6, 16
K = 48
CH = 256
ROOT5 = 5.0**0.5
LOG2E = 1.4426950408889634


def split3(q):
    a = q.astype(jnp.bfloat16)
    r = q - a.astype(jnp.float32)
    b = r.astype(jnp.bfloat16)
    c = (r - b.astype(jnp.float32)).astype(jnp.bfloat16)
    return jnp.concatenate([a, b, c], axis=0)


def tile_kernel(live_ref, list_ref, inv, rows, cols, tiles, rout, cout, w, sem, racc, cacc, lhs, rhs, zi1, zj1, cb):
    live = live_ref[0]

    def fetch(s):
        return pltpu.make_async_copy(tiles.at[s], w.at[s], sem.at[s])

    for s in range(S):

        @pl.when(s < live)
        def _():
            fetch(s).start()

    racc[...] = jnp.zeros(racc.shape, jnp.float32)
    cacc[...] = jnp.zeros(cacc.shape, jnp.float32)
    iv = inv[...]
    ones3 = jnp.ones((3, TB), jnp.bfloat16)
    zpad = jnp.zeros((K - F - 6, TB), jnp.bfloat16)
    onepad = (lax.broadcasted_iota(jnp.int32, (16, TB), 0) == 0).astype(jnp.bfloat16)

    @pl.loop(0, live)
    def _(s):
        big_i = list_ref[2 * s]
        big_j = list_ref[2 * s + 1]
        ib = lax.shift_right_logical(big_i, 4) & 15
        jb = big_j & 15
        scale = jnp.where(big_i == big_j, 1.0, 2.0) * (-5.0 / 3.0 * ROOT5)
        zi = rows[ib]
        zj = cols[jb]
        ui = (iv * zi.astype(jnp.float32)).astype(jnp.bfloat16)
        uj = (iv * zj.astype(jnp.float32)).astype(jnp.bfloat16)
        qi = jnp.sum(jnp.square(ui.astype(jnp.float32)), axis=0, keepdims=True)
        qj = jnp.sum(jnp.square(uj.astype(jnp.float32)), axis=0, keepdims=True)
        lhs[...] = jnp.concatenate([ui, split3(qi), ones3, zpad], axis=0).T
        rhs[...] = jnp.concatenate([uj * jnp.bfloat16(-2.0), ones3, split3(qj), zpad], axis=0)
        zi1[...] = jnp.concatenate([zi, onepad], axis=0)
        zj1[...] = jnp.concatenate([zj, onepad], axis=0)
        fetch(s).wait()
        for jc in range(TB // CH):
            js = pl.ds(jc * CH, CH)
            for ic in range(TB // CH):
                at = pl.ds(ic * CH, CH)
                sq = lax.dot_general(
                    lhs[at, :], rhs[:, js], (((1,), (0,)), ((), ())), preferred_element_type=jnp.float32
                )
                sq = jnp.maximum(sq, 1e-30)
                d = sq * lax.rsqrt(sq)
                e = jnp.exp2(d * (-ROOT5 * LOG2E))
                g = ((d + 1.0 / ROOT5) * e).astype(jnp.bfloat16)
                cb[at, js] = g * w[s, at, js]
        x = cb[...]
        rt = lax.dot_general(zj1[...], x, (((1,), (1,)), ((), ())), preferred_element_type=jnp.float32)
        ct = lax.dot_general(zi1[...], x, (((1,), (0,)), ((), ())), preferred_element_type=jnp.float32)
        racc[ib] += scale * (zi.astype(jnp.float32) * rt[F : F + 1] - rt[:F])
        cacc[jb] += scale * (zj.astype(jnp.float32) * ct[F : F + 1] - ct[:F])

    rout[...] = racc[...].astype(jnp.bfloat16)
    cout[...] = cacc[...].astype(jnp.bfloat16)


def tile_pass(live, tile_list, inv, rows, cols, tiles):
    smem = pl.BlockSpec(memory_space=pltpu.SMEM)
    vmem = pl.BlockSpec(memory_space=pltpu.VMEM)
    part = jax.ShapeDtypeStruct((N, F, TB), jnp.bfloat16)
    return pl.pallas_call(
        tile_kernel,
        out_shape=[part, part],
        in_specs=[smem, smem, vmem, vmem, vmem, pl.BlockSpec(memory_space=pl.ANY)],
        out_specs=[vmem, vmem],
        scratch_shapes=[
            pltpu.VMEM((S, TB, TB), jnp.bfloat16),
            pltpu.SemaphoreType.DMA((S,)),
            pltpu.VMEM((N, F, TB), jnp.float32),
            pltpu.VMEM((N, F, TB), jnp.float32),
            pltpu.VMEM((TB, K), jnp.bfloat16),
            pltpu.VMEM((K, TB), jnp.bfloat16),
            pltpu.VMEM((K, TB), jnp.bfloat16),
            pltpu.VMEM((K, TB), jnp.bfloat16),
            pltpu.VMEM((TB, TB), jnp.bfloat16),
        ],
        compiler_params=pltpu.CompilerParams(vmem_limit_bytes=48 * 1024 * 1024),
        name="tile_pass",
    )(live, tile_list, inv, rows, cols, tiles)


def gather(block, axis):
    copies = jnp.broadcast_to(block[None], (N, F, TB))
    return lax.all_to_all(copies, axis, 0, 0, tiled=True)


def scatter_sum(parts, axis):
    got = lax.all_to_all(parts, axis, 0, 0, tiled=True)
    return jnp.sum(got.astype(jnp.float32), axis=0)


def body(features, inv_scales, inverse_tiles, tile_list, live_count):
    mine = features[0, 0]
    rows = gather(mine, "col")
    cols = gather(mine, "row")
    rpart, cpart = tile_pass(
        live_count.reshape(1), tile_list.reshape(2 * S), inv_scales.reshape(F, 1), rows, cols, inverse_tiles[0, 0]
    )
    total = scatter_sum(rpart, "col") + scatter_sum(cpart, "row")
    return (jnp.square(inv_scales)[:, None] * total)[None, None]


def solution(mesh):
    return jax.shard_map(
        body,
        mesh=mesh,
        in_specs=(
            P("col", "row", None, None),
            P(),
            P("row", "col", None, None, None),
            P("row", "col", None, None),
            P("row", "col"),
        ),
        out_specs=P("col", "row", None, None),
        check_vma=False,
    )
```

time: 453 us -> 134 us (0.30)
  waiting for transfers between devices: 385 us -> 54 us
  blocking collectives: 0 us -> 41.9 us
  matrix products: 26.6 us -> 0 us
  Pallas kernels: 0 us -> 19.3 us
  loops' own time: 15.7 us -> 0 us
  starting transfers between devices: 0.12 us -> 14.3 us
  between operations: 13.2 us -> 0.71 us
    reduce_scatter x2 -> x0, waiting for transfers between devices: 197 us -> none  [the longest x1 121 us: body(): row_part = lax.psum_scatter(row_acc, 'col', scatter_dimension=0, tiled=True)]
    all_gather x2 -> x0, waiting for transfers between devices: 187 us -> none  [the longest x1 113 us: body(): everything = lax.all_gather(column_set[None], 'col', axis=0, tiled=True)]
    all_to_all x0 -> x2, waiting for transfers between devices: none -> 54 us  [the longest x1 27.4 us: scatter_sum(): got = lax.all_to_all(parts, axis, 0, 0, tiled=True)]
    all_to_all x0 -> x2, blocking collectives: none -> 41.9 us  [the longest x1 22.3 us: gather(): return lax.all_to_all(copies, axis, 0, 0, tiled=True)]
    dot_general x9 -> x0, matrix products: 26.6 us -> none  [the longest x3 15.7 us: one_tile(): lax.dot_general(ui, uj, (((0,), (0,)), ((), ())), preferred_element_type=...]
    pallas_call x0 -> x1, Pallas kernels: none -> 19.3 us  [tile_pass(): pl.pallas_call(tile_kernel, out_shape=[part, part], in_specs=[smem, smem,...]
    another operation x1 -> x0, loops' own time: 15.7 us -> none  [body(): row_acc, col_acc = lax.fori_loop(0, live, one_tile, (row_start, col_start))]
    all_to_all x0 -> x2, starting transfers between devices: none -> 14.3 us  [the longest x1 9.29 us: gather(): return lax.all_to_all(copies, axis, 0, 0, tiled=True)]
  transfers between devices with their start and end apart: 4 -> 2, of which waited for: 4 -> 2; matrix products, arithmetic and copies ran while one was open for 0% -> 0% of each run, Pallas kernels for 0% -> 0%
where the time goes in v1:
time: 134 us
  waiting for transfers between devices  54 us (40%)
  blocking collectives  41.9 us (31%)
  Pallas kernels  19.3 us (14%)
  starting transfers between devices  14.3 us (11%)
  local copies, waits for them, and re-layouts  2.21 us (2%)
    all_to_all x1, waiting for transfers between devices, scatter_sum(): got = lax.all_to_all(parts, axis, 0, 0, tiled=True)  27.4 us
    all_to_all x1, waiting for transfers between devices, gather(): return lax.all_to_all(copies, axis, 0, 0, tiled=True)  26.7 us
    all_to_all x1, blocking collectives, gather(): return lax.all_to_all(copies, axis, 0, 0, tiled=True)  22.3 us
    all_to_all x1, blocking collectives, scatter_sum(): got = lax.all_to_all(parts, axis, 0, 0, tiled=True)  19.6 us
    pallas_call x1, Pallas kernels, tile_pass(): pl.pallas_call(tile_kernel, out_shape=[part, part], in_specs=[smem, smem,...  19.3 us
    all_to_all x1, starting transfers between devices, gather(): return lax.all_to_all(copies, axis, 0, 0, tiled=True)  9.29 us
    all_to_all x1, starting transfers between devices, scatter_sum(): got = lax.all_to_all(parts, axis, 0, 0, tiled=True)  5.05 us
  transfers between devices with their start and end apart: 2, of which 2 were waited for; matrix products, arithmetic and copies ran while one was open for 0% of the time, Pallas kernels for 0%

profile of v1, /device:TPU:16, one launch (start us, length us, event | category | flops | bytes accessed | tf_op | source)
XLA Modules:
  0.0 133.6 jit_solution(8417260678335339726)
XLA Ops:
  0.0 1.9 %broadcast_in_dim.5 = bf16[16,32,1024]{2,1,0:T(8,128)(2,1)} broadcast(bf16[32,1024]{1,0:T(8,128)(2,1)} %bitcast.8), dimensions={1,2} | broadcast | bytes 1114112 | tf_op jit(solution)/shard_map/broadcast_in_dim | solution.py:108
  1.9 0.0 copy-start.1
  1.9 0.0 copy-start
  1.9 22.3 %all_to_all.20.rows = bf16[16,32,1024]{2,1,0:T(8,128)(2,1)S(1)} all-to-all(bf16[16,32,1024]{2,1,0:T(8,128)(2,1)} %broadcast_in_dim.5), channel_id=1, replica_groups=mesh['row'=16,'col'=16] {'col'}, dimensions={0} | all-to-all | bytes 2097152 | tf_op jit(solution)/shard_map/all_to_all | solution.py:109
  24.3 9.3 %all-to-all-start.1 = ((bf16[16,32,1024]{2,1,0:T(8,128)(2,1)}), bf16[16,32,1024]{2,1,0:T(8,128)(2,1)S(1)}, u32[]{:S(2)}, u32[]{:S(2)}) async-start(bf16[16,32,1024]{2,1,0:T(8,128)(2,1)} %broadcast_in_dim.5), calls=%async_computation.1 | async-start | bytes 2097152 | tf_op jit(solution)/shard_map/all_to_all | solution.py:109
  33.6 0.0 copy-done.1
  33.6 0.1 copy.9.inv
  33.7 0.0 copy-done
  33.7 0.1 copy.8
  33.8 0.1 reshape.44.list_ref
  34.5 26.7 %all-to-all-done.1.cols = bf16[16,32,1024]{2,1,0:T(8,128)(2,1)S(1)} async-done(((bf16[16,32,1024]{2,1,0:T(8,128)(2,1)}), bf16[16,32,1024]{2,1,0:T(8,128)(2,1)S(1)}, u32[]{:S(2)}, u32[]{:S(2)}) %all-to-all-start.1) | async-done | bytes 1048608 | tf_op jit(solution)/shard_map/all_to_all | solution.py:109
  61.2 19.3 %tile_pass.1 = (bf16[16,32,1024]{2,1,0:T(8,128)(2,1)S(1)}, bf16[16,32,1024]{2,1,0:T(8,128)(2,1)}) custom-call(s32[1]{0:T(128)} %bitcast.6.live_ref, s32[12]{0:T(128)S(1)} %reshape.44.list_ref, f32[32,1]{1,0:T(8,128)S(1)} %copy.9.inv, bf16[16,32,1024]{2,1,0:T(8,128)(2,1)S(1)} %all_to_all.20.rows, bf16[16,32,1024]{2,1,0:T(8,128)(2,1)S(1)} %all-to-all-done.1.cols, ...), custom_call_target="tpu_custom_call" | custom-call | tf_op jit(solution)/shard_map/tile_pass/pallas_call | solution.py:86
  80.5 19.6 %all_to_all.21 = bf16[16,32,1024]{2,1,0:T(8,128)(2,1)S(1)} all-to-all(bf16[16,32,1024]{2,1,0:T(8,128)(2,1)S(1)} %get-tuple-element.7), channel_id=1, replica_groups=mesh['row'=16,'col'=16] {'col'}, dimensions={0} | all-to-all | bytes 2097152 | tf_op jit(solution)/shard_map/all_to_all | solution.py:113
  100.0 5.0 %all-to-all-start.3 = ((bf16[16,32,1024]{2,1,0:T(8,128)(2,1)}), bf16[16,32,1024]{2,1,0:T(8,128)(2,1)S(1)}, u32[]{:S(2)}, u32[]{:S(2)}) async-start(bf16[16,32,1024]{2,1,0:T(8,128)(2,1)} %get-tuple-element.8), calls=%async_computation.3 | async-start | bytes 2097152 | tf_op jit(solution)/shard_map/all_to_all | solution.py:113
  105.1 0.2 convert_reduce_fusion.1
  105.3 27.4 %all-to-all-done.3 = bf16[16,32,1024]{2,1,0:T(8,128)(2,1)S(1)} async-done(((bf16[16,32,1024]{2,1,0:T(8,128)(2,1)}), bf16[16,32,1024]{2,1,0:T(8,128)(2,1)S(1)}, u32[]{:S(2)}, u32[]{:S(2)}) %all-to-all-start.3) | async-done | bytes 1048608 | tf_op jit(solution)/shard_map/all_to_all | solution.py:113
  132.7 0.2 convert_reduce_fusion
  132.9 0.7 bitcast_multiply_fusion
  (1 shorter events, 0.0 us)
Async XLA Ops:
  1.9 31.6 %copy-start.1 = (f32[32]{0:T(128)S(1)}, f32[32]{0:T(128)}, u32[]{:S(2)}) copy-start(f32[32]{0:T(128)} %param.6) | copy-start | bytes 388
  1.9 31.7 %copy-start = (s32[1,1,6,2]{2,3,1,0:T(2,128)S(1)}, s32[1,1,6,2]{2,3,1,0:T(2,128)}, u32[]{:S(2)}) copy-start(s32[1,1,6,2]{2,3,1,0:T(2,128)} %param.8) | copy-start | bytes 148
  24.3 36.9 %all-to-all-start.1 = ((bf16[16,32,1024]{2,1,0:T(8,128)(2,1)}), bf16[16,32,1024]{2,1,0:T(8,128)(2,1)S(1)}, u32[]{:S(2)}, u32[]{:S(2)}) async-start(bf16[16,32,1024]{2,1,0:T(8,128)(2,1)} %broadcast_in_dim.5), calls=%async_computation.1 | async-start | bytes 2097152 | tf_op jit(solution)/shard_map/all_to_all | solution.py:109
  100.0 32.6 %all-to-all-start.3 = ((bf16[16,32,1024]{2,1,0:T(8,128)(2,1)}), bf16[16,32,1024]{2,1,0:T(8,128)(2,1)S(1)}, u32[]{:S(2)}, u32[]{:S(2)}) async-start(bf16[16,32,1024]{2,1,0:T(8,128)(2,1)} %get-tuple-element.8), calls=%async_computation.3 | async-start | bytes 2097152 | tf_op jit(solution)/shard_map/all_to_all | solution.py:113

commit v2 on v1

--- a/solution.py
+++ b/solution.py
@@ -6,6 +6,7 @@
 from jax.sharding import PartitionSpec as P
 
 F, TB, S, N = 32, 1024, 6, 16
+HALF = N // 2
 K = 48
 CH = 256
 ROOT5 = 5.0**0.5
@@ -20,7 +21,8 @@
     return jnp.concatenate([a, b, c], axis=0)
 
 
-def tile_kernel(live_ref, list_ref, inv, rows, cols, tiles, rout, cout, w, sem, racc, cacc, lhs, rhs, zi1, zj1, cb):
+def tile_kernel(live_ref, list_ref, inv, rows, rows2, cols, tiles, rout, rout2, cout, w, sem, racc, cacc, lhs, rhs, zi1, zj1, cb):
+    me = lax.axis_index("col")
     live = live_ref[0]
 
     def fetch(s):
@@ -39,14 +41,28 @@
     zpad = jnp.zeros((K - F - 6, TB), jnp.bfloat16)
     onepad = (lax.broadcasted_iota(jnp.int32, (16, TB), 0) == 0).astype(jnp.bfloat16)
 
+    zi1[F:] = onepad
+    zj1[F:] = onepad
+
     @pl.loop(0, live)
     def _(s):
         big_i = list_ref[2 * s]
         big_j = list_ref[2 * s + 1]
-        ib = lax.shift_right_logical(big_i, 4) & 15
+        owner = lax.shift_right_logical(big_i, 4) & 15
+        ib = col_slot(owner, me)
         jb = big_j & 15
         scale = jnp.where(big_i == big_j, 1.0, 2.0) * (-5.0 / 3.0 * ROOT5)
-        zi = rows[ib]
+        mine = ib < HALF
+
+        @pl.when(mine)
+        def _():
+            zi1[:F] = rows[ib & 7]
+
+        @pl.when(jnp.logical_not(mine))
+        def _():
+            zi1[:F] = rows2[ib & 7]
+
+        zi = zi1[:F]
         zj = cols[jb]
         ui = (iv * zi.astype(jnp.float32)).astype(jnp.bfloat16)
         uj = (iv * zj.astype(jnp.float32)).astype(jnp.bfloat16)
@@ -54,8 +70,7 @@
         qj = jnp.sum(jnp.square(uj.astype(jnp.float32)), axis=0, keepdims=True)
         lhs[...] = jnp.concatenate([ui, split3(qi), ones3, zpad], axis=0).T
         rhs[...] = jnp.concatenate([uj * jnp.bfloat16(-2.0), ones3, split3(qj), zpad], axis=0)
-        zi1[...] = jnp.concatenate([zi, onepad], axis=0)
-        zj1[...] = jnp.concatenate([zj, onepad], axis=0)
+        zj1[:F] = zj
         fetch(s).wait()
         for jc in range(TB // CH):
             js = pl.ds(jc * CH, CH)
@@ -75,19 +90,21 @@
         racc[ib] += scale * (zi.astype(jnp.float32) * rt[F : F + 1] - rt[:F])
         cacc[jb] += scale * (zj.astype(jnp.float32) * ct[F : F + 1] - ct[:F])
 
-    rout[...] = racc[...].astype(jnp.bfloat16)
+    rout[...] = racc[:HALF].astype(jnp.bfloat16)
+    rout2[...] = racc[HALF:].astype(jnp.bfloat16)
     cout[...] = cacc[...].astype(jnp.bfloat16)
 
 
-def tile_pass(live, tile_list, inv, rows, cols, tiles):
+def tile_pass(live, tile_list, inv, rows, rows2, cols, tiles):
     smem = pl.BlockSpec(memory_space=pltpu.SMEM)
     vmem = pl.BlockSpec(memory_space=pltpu.VMEM)
+    half = jax.ShapeDtypeStruct((HALF, F, TB), jnp.bfloat16)
     part = jax.ShapeDtypeStruct((N, F, TB), jnp.bfloat16)
     return pl.pallas_call(
         tile_kernel,
-        out_shape=[part, part],
-        in_specs=[smem, smem, vmem, vmem, vmem, pl.BlockSpec(memory_space=pl.ANY)],
-        out_specs=[vmem, vmem],
+        out_shape=[half, half, part],
+        in_specs=[smem, smem, vmem, vmem, vmem, vmem, pl.BlockSpec(memory_space=pl.ANY)],
+        out_specs=[vmem, vmem, vmem],
         scratch_shapes=[
             pltpu.VMEM((S, TB, TB), jnp.bfloat16),
             pltpu.SemaphoreType.DMA((S,)),
@@ -101,27 +118,54 @@
         ],
         compiler_params=pltpu.CompilerParams(vmem_limit_bytes=48 * 1024 * 1024),
         name="tile_pass",
-    )(live, tile_list, inv, rows, cols, tiles)
+    )(live, tile_list, inv, rows, rows2, cols, tiles)
 
 
-def gather(block, axis):
-    copies = jnp.broadcast_to(block[None], (N, F, TB))
-    return lax.all_to_all(copies, axis, 0, 0, tiled=True)
+def move(x, to):
+    return lax.ppermute(x, "col", [(i, to(i)) for i in range(N)])
 
 
-def scatter_sum(parts, axis):
-    got = lax.all_to_all(parts, axis, 0, 0, tiled=True)
+def along(k):
+    return lambda i: (i + 4 * k) % N
+
+
+def col_slot(owner, me):
+    return ((owner ^ me) & 1) * HALF + (((me - owner + (owner & 3) - (me & 3)) & 12) >> 1) + (((owner ^ me) >> 1) & 1)
+
+
+def gather_col(block):
+    pair = jnp.stack([block, move(block, lambda i: i ^ 2)])
+    mine = jnp.concatenate([pair] + [move(pair, along(k)) for k in (1, 2, 3)])
+    return mine, move(mine, lambda i: i ^ 1)
+
+
+def scatter_col(mine, other):
+    f32, bf16 = jnp.float32, jnp.bfloat16
+    chip = (mine.astype(f32) + move(other, lambda i: i ^ 1).astype(f32)).astype(bf16)
+    pair = chip[:2].astype(f32)
+    for k in (1, 2, 3):
+        pair += move(chip[2 * k : 2 * k + 2], along(-k)).astype(f32)
+    return pair[0] + move(pair[1].astype(bf16), lambda i: i ^ 2).astype(f32)
+
+
+def gather_row(block):
+    copies = jnp.broadcast_to(block[None], (N, F, TB))
+    return lax.all_to_all(copies, "row", 0, 0, tiled=True)
+
+
+def scatter_row(parts):
+    got = lax.all_to_all(parts, "row", 0, 0, tiled=True)
     return jnp.sum(got.astype(jnp.float32), axis=0)
 
 
 def body(features, inv_scales, inverse_tiles, tile_list, live_count):
-    mine = features[0, 0]
-    rows = gather(mine, "col")
-    cols = gather(mine, "row")
-    rpart, cpart = tile_pass(
-        live_count.reshape(1), tile_list.reshape(2 * S), inv_scales.reshape(F, 1), rows, cols, inverse_tiles[0, 0]
+    block = features[0, 0]
+    cols = gather_row(block)
+    rows, rows2 = gather_col(block)
+    rpart, rpart2, cpart = tile_pass(
+        live_count.reshape(1), tile_list.reshape(2 * S), inv_scales.reshape(F, 1), rows, rows2, cols, inverse_tiles[0, 0]
     )
-    total = scatter_sum(rpart, "col") + scatter_sum(cpart, "row")
+    total = scatter_row(cpart) + scatter_col(rpart, rpart2)
     return (jnp.square(inv_scales)[:, None] * total)[None, None]
 
 

time: 134 us -> 91 us (0.68)
  blocking collectives: 41.9 us -> 0 us
  starting transfers between devices: 14.3 us -> 36.2 us
  waiting for transfers between devices: 54 us -> 38.5 us
  Pallas kernels: 19.3 us -> 8.44 us
  local copies, waits for them, and re-layouts: 2.21 us -> 4.5 us
    all_to_all x2 -> x0, blocking collectives: 41.9 us -> none  [the longest x1 22.3 us: gather(): return lax.all_to_all(copies, axis, 0, 0, tiled=True)]
    all_to_all x2, waiting for transfers between devices: 54 us -> 19.7 us  [the longest x1 12.2 us: scatter_row(): got = lax.all_to_all(parts, 'row', 0, 0, tiled=True)]
    ppermute x0 -> x10, waiting for transfers between devices: none -> 18.8 us  [move(): return lax.ppermute(x, 'col', [(i, to(i)) for i in range(N)])]
    ppermute x0 -> x10, starting transfers between devices: none -> 12.5 us  [move(): return lax.ppermute(x, 'col', [(i, to(i)) for i in range(N)])]
    pallas_call x1, Pallas kernels: 19.3 us -> 8.44 us  [tile_pass(): pl.pallas_call(tile_kernel, out_shape=[half, half, part], in_specs=[smem,...]
    all_to_all x2, starting transfers between devices: 14.3 us -> 23.7 us  [the longest x1 14.4 us: scatter_row(): got = lax.all_to_all(parts, 'row', 0, 0, tiled=True)]
    unnamed x5 -> x7, local copies, waits for them, and re-layouts: 0.1 us -> 1.67 us
  transfers between devices with their start and end apart: 2 -> 12, of which waited for: 2 -> 10; matrix products, arithmetic and copies ran while one was open for 0% -> 4% of each run, Pallas kernels for 0% -> 0%
where the time goes in v2:
time: 91 us; the launch traced here: 90.4 us
  waiting for transfers between devices  38.5 us (42%)
  starting transfers between devices  36.2 us (40%)
  Pallas kernels  8.44 us (9%)
  local copies, waits for them, and re-layouts  4.5 us (5%)
  other arithmetic  2.04 us (2%)
    ppermute x10, waiting for transfers between devices, move(): return lax.ppermute(x, 'col', [(i, to(i)) for i in range(N)])  18.8 us
    all_to_all x1, starting transfers between devices, scatter_row(): got = lax.all_to_all(parts, 'row', 0, 0, tiled=True)  14.4 us
    ppermute x10, starting transfers between devices, move(): return lax.ppermute(x, 'col', [(i, to(i)) for i in range(N)])  12.5 us
    all_to_all x1, waiting for transfers between devices, scatter_row(): got = lax.all_to_all(parts, 'row', 0, 0, tiled=True)  12.2 us
    all_to_all x1, starting transfers between devices, gather_row(): return lax.all_to_all(copies, 'row', 0, 0, tiled=True)  9.29 us
    pallas_call x1, Pallas kernels, tile_pass(): pl.pallas_call(tile_kernel, out_shape=[half, half, part], in_specs=[smem,...  8.44 us
    all_to_all x1, waiting for transfers between devices, gather_row(): return lax.all_to_all(copies, 'row', 0, 0, tiled=True)  7.48 us
    broadcast_in_dim x1, local copies, waits for them, and re-layouts, gather_row(): copies = jnp.broadcast_to(block[None], (N, F, TB))  1.96 us
  transfers between devices with their start and end apart: 12, of which 10 were waited for; matrix products, arithmetic and copies ran while one was open for 4% of the time, Pallas kernels for 0%

profile of v2, /device:TPU:16, one launch (start us, length us, event | category | flops | bytes accessed | tf_op | source)
XLA Modules:
  0.0 90.4 jit_solution(1079955663394315072)
XLA Ops:
  0.0 0.0 copy-start
  0.0 2.0 %broadcast_in_dim.4 = bf16[16,32,1024]{2,1,0:T(8,128)(2,1)} broadcast(bf16[32,1024]{1,0:T(8,128)(2,1)} %bitcast.24), dimensions={1,2} | broadcast | bytes 1114112 | tf_op jit(solution)/shard_map/broadcast_in_dim | solution.py:152
  2.0 9.3 %all-to-all-start = ((bf16[16,32,1024]{2,1,0:T(8,128)(2,1)}), bf16[16,32,1024]{2,1,0:T(8,128)(2,1)S(1)}, u32[]{:S(2)}, u32[]{:S(2)}) async-start(bf16[16,32,1024]{2,1,0:T(8,128)(2,1)} %broadcast_in_dim.4), calls=%async_computation | async-start | bytes 2097152 | tf_op jit(solution)/shard_map/all_to_all | solution.py:153
  11.3 0.7 collective-permute-start
  12.0 0.9 constant_dynamic-update-slice_fusion.4
  12.9 5.5 %collective-permute-done = bf16[32,1024]{1,0:T(8,128)(2,1)S(1)} collective-permute-done((bf16[32,1024]{1,0:T(8,128)(2,1)}, bf16[32,1024]{1,0:T(8,128)(2,1)S(1)}, u32[]{:S(2)}, u32[]{:S(2)}) %collective-permute-start) | collective-permute-done | bytes 65568 | tf_op jit(solution)/shard_map/ppermute | solution.py:125
  18.4 0.9 pad_maximum_fusion
  19.2 1.6 %collective-permute-start.1 = (bf16[2,32,1024]{2,1,0:T(8,128)(2,1)S(1)}, bf16[2,32,1024]{2,1,0:T(8,128)(2,1)S(1)}, u32[]{:S(2)}, u32[]{:S(2)}) collective-permute-start(bf16[2,32,1024]{2,1,0:T(8,128)(2,1)S(1)} %pad_maximum_fusion), channel_id=1, source_target_pairs={{0,4},{1,5},{2,6},{3,7},{4,8},{5,9},{6,10},{7,11},{8,12},{9,13},{1... | collective-permute-start | bytes 393224 | tf_op jit(solution)/shard_map/ppermute | solution.py:125
  20.8 2.7 %collective-permute-start.2 = (bf16[2,32,1024]{2,1,0:T(8,128)(2,1)S(1)}, bf16[2,32,1024]{2,1,0:T(8,128)(2,1)S(1)}, u32[]{:S(2)}, u32[]{:S(2)}) collective-permute-start(bf16[2,32,1024]{2,1,0:T(8,128)(2,1)S(1)} %pad_maximum_fusion), channel_id=1, source_target_pairs={{0,8},{1,9},{2,10},{3,11},{4,12},{5,13},{6,14},{7,15},{8,0},{9,1},... | collective-permute-start | bytes 393224 | tf_op jit(solution)/shard_map/ppermute | solution.py:125
  23.5 1.4 %collective-permute-start.3 = (bf16[2,32,1024]{2,1,0:T(8,128)(2,1)S(1)}, bf16[2,32,1024]{2,1,0:T(8,128)(2,1)S(1)}, u32[]{:S(2)}, u32[]{:S(2)}) collective-permute-start(bf16[2,32,1024]{2,1,0:T(8,128)(2,1)S(1)} %pad_maximum_fusion), channel_id=1, source_target_pairs={{0,12},{1,13},{2,14},{3,15},{4,0},{5,1},{6,2},{7,3},{8,4},{9,5},{1... | collective-permute-start | bytes 393224 | tf_op jit(solution)/shard_map/ppermute | solution.py:125
  25.0 1.1 %collective-permute-done.1 = bf16[2,32,1024]{2,1,0:T(8,128)(2,1)S(1)} collective-permute-done((bf16[2,32,1024]{2,1,0:T(8,128)(2,1)S(1)}, bf16[2,32,1024]{2,1,0:T(8,128)(2,1)S(1)}, u32[]{:S(2)}, u32[]{:S(2)}) %collective-permute-start.1) | collective-permute-done | bytes 131104 | tf_op jit(solution)/shard_map/ppermute | solution.py:125
  26.1 1.8 %collective-permute-done.2 = bf16[2,32,1024]{2,1,0:T(8,128)(2,1)S(1)} collective-permute-done((bf16[2,32,1024]{2,1,0:T(8,128)(2,1)S(1)}, bf16[2,32,1024]{2,1,0:T(8,128)(2,1)S(1)}, u32[]{:S(2)}, u32[]{:S(2)}) %collective-permute-start.2) | collective-permute-done | bytes 131104 | tf_op jit(solution)/shard_map/ppermute | solution.py:125
  27.9 0.6 collective-permute-done.3
  28.5 0.1 collective-permute-start.4
  28.6 0.7 copy.9.inv
  29.3 0.8 copy.8
  30.1 0.1 reshape.13.list_ref
  30.8 0.0 collective-permute-done.4.rows2
  30.9 7.5 %all-to-all-done.cols = bf16[16,32,1024]{2,1,0:T(8,128)(2,1)S(1)} async-done(((bf16[16,32,1024]{2,1,0:T(8,128)(2,1)}), bf16[16,32,1024]{2,1,0:T(8,128)(2,1)S(1)}, u32[]{:S(2)}, u32[]{:S(2)}) %all-to-all-start) | async-done | bytes 1048608 | tf_op jit(solution)/shard_map/all_to_all | solution.py:153
  38.3 8.4 %tile_pass.1 = (bf16[8,32,1024]{2,1,0:T(8,128)(2,1)S(1)}, bf16[8,32,1024]{2,1,0:T(8,128)(2,1)S(1)}, bf16[16,32,1024]{2,1,0:T(8,128)(2,1)}) custom-call(s32[1]{0:T(128)} %bitcast.22.live_ref, s32[12]{0:T(128)S(1)} %reshape.13.list_ref, f32[32,1]{1,0:T(8,128)S(1)} %copy.9.inv, bf16[8,32,1024]{2,1,0:T(8,128)(2,1)S(1)} %constant_dynamic-update-slice_fusion.rows, ...), custom_call_target="tpu_custom_call" | custom-call | tf_op jit(solution)/shard_map/tile_pass/pallas_call | solution.py:103
  46.8 14.4 %all-to-all-start.1 = ((bf16[16,32,1024]{2,1,0:T(8,128)(2,1)}), bf16[16,32,1024]{2,1,0:T(8,128)(2,1)S(1)}, u32[]{:S(2)}, u32[]{:S(2)}) async-start(bf16[16,32,1024]{2,1,0:T(8,128)(2,1)} %get-tuple-element.8), calls=%async_computation.1 | async-start | bytes 2097152 | tf_op jit(solution)/shard_map/all_to_all | solution.py:157
  61.2 0.7 collective-permute-start.5
  61.9 1.5 %collective-permute-done.5 = bf16[8,32,1024]{2,1,0:T(8,128)(2,1)S(1)} collective-permute-done((bf16[8,32,1024]{2,1,0:T(8,128)(2,1)S(1)}, bf16[8,32,1024]{2,1,0:T(8,128)(2,1)S(1)}, u32[]{:S(2)}, u32[]{:S(2)}) %collective-permute-start.5) | collective-permute-done | bytes 524320 | tf_op jit(solution)/shard_map/ppermute | solution.py:125
  63.4 0.2 add_convert_fusion
  63.6 3.2 %collective-permute-start.6 = (bf16[2,32,1024]{2,1,0:T(8,128)(2,1)S(1)}, bf16[2,32,1024]{2,1,0:T(8,128)(2,1)S(1)}, u32[]{:S(2)}, u32[]{:S(2)}) collective-permute-start(bf16[2,32,1024]{2,1,0:T(8,128)(2,1)S(1)} %get-tuple-element.11), channel_id=1, source_target_pairs={{0,12},{1,13},{2,14},{3,15},{4,0},{5,1},{6,2},{7,3},{8,4},{9,5},{1... | collective-permute-start | bytes 393224 | tf_op jit(solution)/shard_map/ppermute | solution.py:125
  66.8 1.1 %collective-permute-start.7 = (bf16[2,32,1024]{2,1,0:T(8,128)(2,1)S(1)}, bf16[2,32,1024]{2,1,0:T(8,128)(2,1)S(1)}, u32[]{:S(2)}, u32[]{:S(2)}) collective-permute-start(bf16[2,32,1024]{2,1,0:T(8,128)(2,1)S(1)} %get-tuple-element.13), channel_id=1, source_target_pairs={{0,8},{1,9},{2,10},{3,11},{4,12},{5,13},{6,14},{7,15},{8,0},{9,1},... | collective-permute-start | bytes 393224 | tf_op jit(solution)/shard_map/ppermute | solution.py:125
  67.9 0.2 collective-permute-start.8
  68.2 0.0 copy-done
  68.2 4.6 %collective-permute-done.6 = bf16[2,32,1024]{2,1,0:T(8,128)(2,1)S(1)} collective-permute-done((bf16[2,32,1024]{2,1,0:T(8,128)(2,1)S(1)}, bf16[2,32,1024]{2,1,0:T(8,128)(2,1)S(1)}, u32[]{:S(2)}, u32[]{:S(2)}) %collective-permute-start.6) | collective-permute-done | bytes 131104 | tf_op jit(solution)/shard_map/ppermute | solution.py:125
  72.7 2.0 %collective-permute-done.7 = bf16[2,32,1024]{2,1,0:T(8,128)(2,1)S(1)} collective-permute-done((bf16[2,32,1024]{2,1,0:T(8,128)(2,1)S(1)}, bf16[2,32,1024]{2,1,0:T(8,128)(2,1)S(1)}, u32[]{:S(2)}, u32[]{:S(2)}) %collective-permute-start.7) | collective-permute-done | bytes 131104 | tf_op jit(solution)/shard_map/ppermute | solution.py:125
  74.7 1.7 %collective-permute-done.8 = bf16[2,32,1024]{2,1,0:T(8,128)(2,1)S(1)} collective-permute-done((bf16[2,32,1024]{2,1,0:T(8,128)(2,1)S(1)}, bf16[2,32,1024]{2,1,0:T(8,128)(2,1)S(1)}, u32[]{:S(2)}, u32[]{:S(2)}) %collective-permute-start.8) | collective-permute-done | bytes 131104 | tf_op jit(solution)/shard_map/ppermute | solution.py:125
  76.4 0.1 convert_add_fusion
  76.5 0.7 collective-permute-start.9
  77.2 12.2 %all-to-all-done.1 = bf16[16,32,1024]{2,1,0:T(8,128)(2,1)S(1)} async-done(((bf16[16,32,1024]{2,1,0:T(8,128)(2,1)}), bf16[16,32,1024]{2,1,0:T(8,128)(2,1)S(1)}, u32[]{:S(2)}, u32[]{:S(2)}) %all-to-all-start.1) | async-done | bytes 1048608 | tf_op jit(solution)/shard_map/all_to_all | solution.py:157
  89.4 0.2 convert_reduce_fusion
  89.6 0.0 collective-permute-done.9
  89.6 0.7 fusion.3
  (7 shorter events, 0.1 us)
Async XLA Ops:
  0.0 68.2 %copy-start = (f32[32]{0:T(128)S(1)}, f32[32]{0:T(128)}, u32[]{:S(2)}) copy-start(f32[32]{0:T(128)} %param.6) | copy-start | bytes 388
  2.0 36.4 %all-to-all-start = ((bf16[16,32,1024]{2,1,0:T(8,128)(2,1)}), bf16[16,32,1024]{2,1,0:T(8,128)(2,1)S(1)}, u32[]{:S(2)}, u32[]{:S(2)}) async-start(bf16[16,32,1024]{2,1,0:T(8,128)(2,1)} %broadcast_in_dim.4), calls=%async_computation | async-start | bytes 2097152 | tf_op jit(solution)/shard_map/all_to_all | solution.py:153
  11.3 7.1 %collective-permute-start = (bf16[32,1024]{1,0:T(8,128)(2,1)}, bf16[32,1024]{1,0:T(8,128)(2,1)S(1)}, u32[]{:S(2)}, u32[]{:S(2)}) collective-permute-start(bf16[32,1024]{1,0:T(8,128)(2,1)} %bitcast.25), channel_id=1, source_target_pairs={{0,2},{1,3},{2,0},{3,1},{4,6},{5,7},{6,4},{7,5},{8,10},{9,11},{10,... | collective-permute-start | bytes 196616 | tf_op jit(solution)/shard_map/ppermute | solution.py:125
  19.2 6.8 %collective-permute-start.1 = (bf16[2,32,1024]{2,1,0:T(8,128)(2,1)S(1)}, bf16[2,32,1024]{2,1,0:T(8,128)(2,1)S(1)}, u32[]{:S(2)}, u32[]{:S(2)}) collective-permute-start(bf16[2,32,1024]{2,1,0:T(8,128)(2,1)S(1)} %pad_maximum_fusion), channel_id=1, source_target_pairs={{0,4},{1,5},{2,6},{3,7},{4,8},{5,9},{6,10},{7,11},{8,12},{9,13},{1... | collective-permute-start | bytes 393224 | tf_op jit(solution)/shard_map/ppermute | solution.py:125
  20.8 7.1 %collective-permute-start.2 = (bf16[2,32,1024]{2,1,0:T(8,128)(2,1)S(1)}, bf16[2,32,1024]{2,1,0:T(8,128)(2,1)S(1)}, u32[]{:S(2)}, u32[]{:S(2)}) collective-permute-start(bf16[2,32,1024]{2,1,0:T(8,128)(2,1)S(1)} %pad_maximum_fusion), channel_id=1, source_target_pairs={{0,8},{1,9},{2,10},{3,11},{4,12},{5,13},{6,14},{7,15},{8,0},{9,1},... | collective-permute-start | bytes 393224 | tf_op jit(solution)/shard_map/ppermute | solution.py:125
  23.5 5.0 %collective-permute-start.3 = (bf16[2,32,1024]{2,1,0:T(8,128)(2,1)S(1)}, bf16[2,32,1024]{2,1,0:T(8,128)(2,1)S(1)}, u32[]{:S(2)}, u32[]{:S(2)}) collective-permute-start(bf16[2,32,1024]{2,1,0:T(8,128)(2,1)S(1)} %pad_maximum_fusion), channel_id=1, source_target_pairs={{0,12},{1,13},{2,14},{3,15},{4,0},{5,1},{6,2},{7,3},{8,4},{9,5},{1... | collective-permute-start | bytes 393224 | tf_op jit(solution)/shard_map/ppermute | solution.py:125
  28.5 2.3 %collective-permute-start.4 = (bf16[8,32,1024]{2,1,0:T(8,128)(2,1)S(1)}, bf16[8,32,1024]{2,1,0:T(8,128)(2,1)S(1)}, u32[]{:S(2)}, u32[]{:S(2)}) collective-permute-start(bf16[8,32,1024]{2,1,0:T(8,128)(2,1)S(1)} %constant_dynamic-update-slice_fusion.rows), channel_id=1, source_target_pairs={{0,1},{1,0},{2,3},{3,2},{4,5},{5,4},{6,7},{7,6},{8,9},{9,8},{10,11... | collective-permute-start | bytes 1572872 | tf_op jit(solution)/shard_map/ppermute | solution.py:125
  46.8 42.7 %all-to-all-start.1 = ((bf16[16,32,1024]{2,1,0:T(8,128)(2,1)}), bf16[16,32,1024]{2,1,0:T(8,128)(2,1)S(1)}, u32[]{:S(2)}, u32[]{:S(2)}) async-start(bf16[16,32,1024]{2,1,0:T(8,128)(2,1)} %get-tuple-element.8), calls=%async_computation.1 | async-start | bytes 2097152 | tf_op jit(solution)/shard_map/all_to_all | solution.py:157
  61.2 2.2 %collective-permute-start.5 = (bf16[8,32,1024]{2,1,0:T(8,128)(2,1)S(1)}, bf16[8,32,1024]{2,1,0:T(8,128)(2,1)S(1)}, u32[]{:S(2)}, u32[]{:S(2)}) collective-permute-start(bf16[8,32,1024]{2,1,0:T(8,128)(2,1)S(1)} %get-tuple-element.10), channel_id=1, source_target_pairs={{0,1},{1,0},{2,3},{3,2},{4,5},{5,4},{6,7},{7,6},{8,9},{9,8},{10,11... | collective-permute-start | bytes 1572872 | tf_op jit(solution)/shard_map/ppermute | solution.py:125
  63.6 9.1 %collective-permute-start.6 = (bf16[2,32,1024]{2,1,0:T(8,128)(2,1)S(1)}, bf16[2,32,1024]{2,1,0:T(8,128)(2,1)S(1)}, u32[]{:S(2)}, u32[]{:S(2)}) collective-permute-start(bf16[2,32,1024]{2,1,0:T(8,128)(2,1)S(1)} %get-tuple-element.11), channel_id=1, source_target_pairs={{0,12},{1,13},{2,14},{3,15},{4,0},{5,1},{6,2},{7,3},{8,4},{9,5},{1... | collective-permute-start | bytes 393224 | tf_op jit(solution)/shard_map/ppermute | solution.py:125
  66.8 7.9 %collective-permute-start.7 = (bf16[2,32,1024]{2,1,0:T(8,128)(2,1)S(1)}, bf16[2,32,1024]{2,1,0:T(8,128)(2,1)S(1)}, u32[]{:S(2)}, u32[]{:S(2)}) collective-permute-start(bf16[2,32,1024]{2,1,0:T(8,128)(2,1)S(1)} %get-tuple-element.13), channel_id=1, source_target_pairs={{0,8},{1,9},{2,10},{3,11},{4,12},{5,13},{6,14},{7,15},{8,0},{9,1},... | collective-permute-start | bytes 393224 | tf_op jit(solution)/shard_map/ppermute | solution.py:125
  67.9 8.5 %collective-permute-start.8 = (bf16[2,32,1024]{2,1,0:T(8,128)(2,1)S(1)}, bf16[2,32,1024]{2,1,0:T(8,128)(2,1)S(1)}, u32[]{:S(2)}, u32[]{:S(2)}) collective-permute-start(bf16[2,32,1024]{2,1,0:T(8,128)(2,1)S(1)} %get-tuple-element.12), channel_id=1, source_target_pairs={{0,4},{1,5},{2,6},{3,7},{4,8},{5,9},{6,10},{7,11},{8,12},{9,13},{1... | collective-permute-start | bytes 393224 | tf_op jit(solution)/shard_map/ppermute | solution.py:125
  76.5 13.1 %collective-permute-start.9 = (bf16[32,1024]{1,0:T(8,128)(2,1)S(1)}, bf16[32,1024]{1,0:T(8,128)(2,1)S(1)}, u32[]{:S(2)}, u32[]{:S(2)}) collective-permute-start(bf16[32,1024]{1,0:T(8,128)(2,1)S(1)} %fusion.4), channel_id=1, source_target_pairs={{0,2},{1,3},{2,0},{3,1},{4,6},{5,7},{6,4},{7,5},{8,10},{9,11},{10,... | collective-permute-start | bytes 196616 | tf_op jit(solution)/shard_map/ppermute | solution.py:125

commit v3 on v2

v3 whole, which is shorter than its diff:
```python
import jax
import jax.numpy as jnp
from jax import lax
from jax.experimental import pallas as pl
from jax.experimental.pallas import tpu as pltpu
from jax.sharding import PartitionSpec as P

F, TB, S, N = 32, 1024, 6, 16
HALF = N // 2
FH = F // 2
TJ = TB // 2
K = 48
SI, SUB, CJ = 512, 128, 256
NS = TB // SI
ROOT5 = 5.0**0.5
LOG2E = 1.4426950408889634
f32, bf16 = jnp.float32, jnp.bfloat16


def nn(a, b):
    return lax.dot_general(a, b, (((1,), (0,)), ((), ())), preferred_element_type=f32)


def nt(a, b):
    return lax.dot_general(a, b, (((1,), (1,)), ((), ())), preferred_element_type=f32)


def split3(q):
    a = q.astype(bf16)
    r = q - a.astype(f32)
    b = r.astype(bf16)
    c = (r - b.astype(f32)).astype(bf16)
    return jnp.concatenate([a, b, c], axis=0)


def scaled(iv, z):
    u = (iv * z.astype(f32)).astype(bf16)
    return u, split3(jnp.sum(jnp.square(u.astype(f32)), axis=0, keepdims=True))


def ones_row(width):
    return (lax.broadcasted_iota(jnp.int32, (K - F, width), 0) == 0).astype(bf16)


def row_place(list_ref, s):
    return col_slot(lax.shift_right_logical(list_ref[2 * s], 4) & 15, lax.axis_index("col"))


def prepare_rows(live_ref, list_ref, inv, near, far, lhs, zi1):
    iv = inv[...]

    @pl.loop(0, live_ref[0])
    def _(s):
        ib = row_place(list_ref, s)

        @pl.when(ib < HALF)
        def _():
            zi1[s, :F] = near[ib & 7]

        @pl.when(ib >= HALF)
        def _():
            zi1[s, :F] = far[ib & 7]

        zi1[s, F:] = ones_row(TB)
        u, q = scaled(iv, zi1[s, :F])
        pad = jnp.zeros((K - F - 6, TB), bf16)
        lhs[s] = jnp.concatenate([u, q, jnp.ones((3, TB), bf16), pad], axis=0).T


def tile_kernel(second, live_ref, list_ref, inv, lhs, zi1, cols, *refs):
    if second:
        swapped, carry, tiles, rout, rout2, cout, w, sem, cacc, rhs, zj1, cb, racc = refs
    else:
        tiles, racc, keep, send, w, sem, cacc, rhs, zj1, cb = refs
    y = lax.axis_index("row") >> 3
    mine, other = pl.multiple_of(y * FH, FH), pl.multiple_of((1 - y) * FH, FH)
    live = live_ref[0]

    def fetch(s):
        return pltpu.make_async_copy(tiles.at[s, :, pl.ds(TJ if second else 0, TJ)], w.at[s], sem.at[s])

    fetch(0).start()

    @pl.when(1 < live)
    def _():
        fetch(1).start()

    racc[...] = jnp.zeros(racc.shape, f32)
    cacc[...] = jnp.zeros(cacc.shape, f32)
    zj1[1] = jnp.zeros((K, TJ), bf16)
    cb[NS - 1] = jnp.zeros((SI, TJ), bf16)
    iv = inv[...]

    def slot(s):
        big_i, big_j = list_ref[2 * s], list_ref[2 * s + 1]
        scale = jnp.where(big_i == big_j, 1.0, 2.0) * (-5.0 / 3.0 * ROOT5)
        return row_place(list_ref, s), big_j & 15, scale

    def prepare(s, p):
        jb = list_ref[2 * s + 1] & 15
        if second:
            zj1[p, pl.ds(mine, FH)] = cols[jb, F:]
            zj1[p, pl.ds(other, FH)] = swapped[jb]
        else:
            zj1[p, :F] = cols[jb, :F]
        zj1[p, F:] = ones_row(TJ)
        u, q = scaled(iv, zj1[p, :F])
        pad = jnp.zeros((K - F - 6, TJ), bf16)
        rhs[p] = jnp.concatenate([u * bf16(-2.0), jnp.ones((3, TJ), bf16), q, pad], axis=0)

    def contract(n, jc, s, p, jb, scale):
        js = pl.ds(jc * CJ, CJ)
        x = cb[n, :, js]
        ct = nn(zi1[s, :, pl.ds(n * SI, SI)], x)
        cacc[jb, :, js] += scale * (zj1[p, :F, js].astype(f32) * ct[F : F + 1] - ct[:F])
        return nt(zj1[p, :, js], x)

    def finish(n, s, ib, scale, rt):
        at = pl.ds(n * SI, SI)
        racc[ib, :, at] += scale * (zi1[s, :F, at].astype(f32) * rt[F : F + 1] - rt[:F])

    prepare(0, 0)

    @pl.loop(0, live)
    def _(s):
        p = s & 1
        prev = jnp.maximum(s - 1, 0)
        now, old = slot(s), slot(prev)
        fetch(s).wait()

        @pl.when(s + 2 < live)
        def _():
            fetch(s + 2).start()

        for n in range(NS):
            m, t, q, (ib, jb, scale) = (n - 1, s, p, now) if n else (NS - 1, prev, 1 - p, old)
            rt = None
            for jc in range(TJ // CJ):
                part = contract(m, jc, t, q, jb, scale)
                rt = part if rt is None else rt + part
                js = pl.ds(jc * CJ, CJ)
                for h in range(SI // SUB):
                    at = pl.ds(n * SI + h * SUB, SUB)
                    sq = jnp.maximum(nn(lhs[s, at, :], rhs[p, :, js]), 1e-30)
                    d = sq * lax.rsqrt(sq)
                    e = jnp.exp2(d * (-ROOT5 * LOG2E))
                    g = ((d + 1.0 / ROOT5) * e).astype(bf16)
                    cb[n, h * SUB : (h + 1) * SUB, js] = g * w[s, at, js]
            finish(m, t, ib, scale, rt)
            if n == NS - 1:
                prepare(jnp.minimum(s + 1, live - 1), 1 - p)

    last = live - 1
    ib, jb, scale = slot(last)
    rt = None
    for jc in range(TJ // CJ):
        part = contract(NS - 1, jc, last, last & 1, jb, scale)
        rt = part if rt is None else rt + part
    finish(NS - 1, last, ib, scale, rt)
    if second:
        rout[...] = (racc[:HALF] + carry[:HALF]).astype(bf16)
        rout2[...] = (racc[HALF:] + carry[HALF:]).astype(bf16)
        cout[:, :F] = cacc[...].astype(bf16)
        cout[:, F:] = jnp.zeros((N, FH, TJ), bf16)
    else:
        keep[...] = cacc[:, pl.ds(mine, FH)]
        send[...] = cacc[:, pl.ds(other, FH)].astype(bf16)


SMEM = pl.BlockSpec(memory_space=pltpu.SMEM)
VMEM = pl.BlockSpec(memory_space=pltpu.VMEM)


def prepare_pass(live, tile_list, inv, near, far):
    return pl.pallas_call(
        prepare_rows,
        out_shape=[jax.ShapeDtypeStruct((S, TB, K), bf16), jax.ShapeDtypeStruct((S, K, TB), bf16)],
        in_specs=[SMEM, SMEM] + [VMEM] * 3,
        out_specs=[VMEM] * 2,
        compiler_params=pltpu.CompilerParams(vmem_limit_bytes=16 * 1024 * 1024),
        cost_estimate=pl.CostEstimate(flops=2 * 10**9, bytes_accessed=10**6, transcendentals=0),
        name="prepare_rows",
    )(live, tile_list, inv, near, far)


def tile_pass(second, tiles, *args):
    total = (N, F, TB)
    half = jax.ShapeDtypeStruct((HALF, F, TB), bf16)
    scratch = [
        pltpu.VMEM((S, TB, TJ), bf16),
        pltpu.SemaphoreType.DMA((S,)),
        pltpu.VMEM((N, F, TJ), f32),
        pltpu.VMEM((2, K, TJ), bf16),
        pltpu.VMEM((2, K, TJ), bf16),
        pltpu.VMEM((NS, SI, TJ), bf16),
    ]
    if second:
        outs = [half, half, jax.ShapeDtypeStruct((N, F + FH, TJ), bf16)]
        scratch.append(pltpu.VMEM(total, f32))
    else:
        outs = [jax.ShapeDtypeStruct(shape, t) for shape, t in ((total, f32), ((N, FH, TJ), f32), ((N, FH, TJ), bf16))]

    def run(*refs):
        tile_kernel(second, *refs)

    return pl.pallas_call(
        run,
        out_shape=outs,
        in_specs=[SMEM] * 2 + [VMEM] * (len(args) - 2) + [pl.BlockSpec(memory_space=pl.ANY)],
        out_specs=[VMEM] * len(outs),
        scratch_shapes=scratch,
        compiler_params=pltpu.CompilerParams(vmem_limit_bytes=44 * 1024 * 1024),
        cost_estimate=pl.CostEstimate(flops=10**10, bytes_accessed=10**7, transcendentals=0),
        name="second_half" if second else "first_half",
    )(*args, tiles)


def move(x, to):
    return lax.ppermute(x, "col", [(i, to(i)) for i in range(N)])


def along(k):
    return lambda i: (i + 4 * k) % N


def col_slot(owner, me):
    return ((owner ^ me) & 1) * HALF + (((me - owner + (owner & 3) - (me & 3)) & 12) >> 1) + (((owner ^ me) >> 1) & 1)


def gather_col(block):
    pair = jnp.stack([block, move(block, lambda i: i ^ 2)])
    mine = jnp.concatenate([pair] + [move(pair, along(k)) for k in (1, 2, 3)])
    return mine, move(mine, lambda i: i ^ 1)


def scatter_col(mine, other):
    chip = (mine.astype(f32) + move(other, lambda i: i ^ 1).astype(f32)).astype(bf16)
    pair = chip[:2].astype(f32)
    for k in (1, 2, 3):
        pair += move(chip[2 * k : 2 * k + 2], along(-k)).astype(f32)
    return pair[0] + move(pair[1].astype(bf16), lambda i: i ^ 2).astype(f32)


def swap_y(x):
    return lax.ppermute(x, "row", [(i, i ^ HALF) for i in range(N)])


def gather_row(block):
    whole = jnp.broadcast_to(block[None, :, :TJ], (2, F, TJ))
    part = block[:, TJ:].reshape(2, FH, TJ)
    copies = jnp.concatenate([whole, part], axis=1)
    copies = jnp.broadcast_to(copies[:, None], (2, HALF, F + FH, TJ)).reshape(N, F + FH, TJ)
    return lax.all_to_all(copies, "row", 0, 0, tiled=True)


def scatter_row(parts):
    got = lax.all_to_all(parts, "row", 0, 0, tiled=True).astype(f32)
    second = jnp.sum(got[:, :F], axis=0)
    first = jnp.sum(got[:, F:].reshape(2, HALF, FH, TJ), axis=1).reshape(F, TJ)
    return jnp.concatenate([first, second], axis=1)


def body(features, inv_scales, inverse_tiles, tile_list, live_count):
    block = features[0, 0]
    live, places, inv = live_count.reshape(1), tile_list.reshape(2 * S), inv_scales.reshape(F, 1)
    cols = gather_row(block)
    near, far = gather_col(block)
    lhs, zi1 = prepare_pass(live, places, inv, near, far)
    swapped = swap_y(cols[:, F:])
    tiles = inverse_tiles[0, 0]
    carry, keep, send = tile_pass(False, tiles, live, places, inv, lhs, zi1, cols)
    got = swap_y(send)
    rpart, rpart2, cpart = tile_pass(True, tiles, live, places, inv, lhs, zi1, cols, swapped, carry)
    pair = (keep + got.astype(f32)).astype(bf16)
    cpart = lax.dynamic_update_slice(cpart, pair, (0, F, 0))
    total = scatter_row(cpart) + scatter_col(rpart, rpart2)
    return (jnp.square(inv_scales)[:, None] * total)[None, None]


def solution(mesh):
    return jax.shard_map(
        body,
        mesh=mesh,
        in_specs=(
            P("col", "row", None, None),
            P(),
            P("row", "col", None, None, None),
            P("row", "col", None, None),
            P("row", "col"),
        ),
        out_specs=P("col", "row", None, None),
        check_vma=False,
    )
```

time: 91 us -> 84.8 us (0.932)
  the two profiles are of different devices: /device:TPU:16 before, /device:TPU:4 now
where the time goes in v3:
time: 84.8 us
  starting transfers between devices  34.2 us (40%)
  waiting for transfers between devices  33 us (39%)
  Pallas kernels  10.6 us (12%)
  local copies, waits for them, and re-layouts  4.01 us (5%)
  other arithmetic  2.13 us (3%)
  between operations  0.87 us (1%)
    ppermute x10, starting transfers between devices, move(): return lax.ppermute(x, 'col', [(i, to(i)) for i in range(N)])  13.1 us
    ppermute x10, waiting for transfers between devices, move(): return lax.ppermute(x, 'col', [(i, to(i)) for i in range(N)])  13 us
    all_to_all x1, waiting for transfers between devices, scatter_row(): got = lax.all_to_all(parts, 'row', 0, 0, tiled=True).astype(f32)  12.6 us
    pallas_call x2, Pallas kernels, tile_pass(): pl.pallas_call(run, out_shape=outs, in_specs=[SMEM] * 2 + [VMEM] * (len(a...  9.63 us
    all_to_all x1, starting transfers between devices, scatter_row(): got = lax.all_to_all(parts, 'row', 0, 0, tiled=True).astype(f32)  8.99 us
    all_to_all x1, starting transfers between devices, gather_row(): return lax.all_to_all(copies, 'row', 0, 0, tiled=True)  8.81 us
    all_to_all x1, waiting for transfers between devices, gather_row(): return lax.all_to_all(copies, 'row', 0, 0, tiled=True)  7.39 us
    ppermute x2, starting transfers between devices, swap_y(): return lax.ppermute(x, 'row', [(i, i ^ HALF) for i in range(N)])  3.22 us
  transfers between devices with their start and end apart: 14, of which 9 were waited for; matrix products, arithmetic and copies ran while one was open for 4% of the time, Pallas kernels for 13%

profile of v3, /device:TPU:4, one launch (start us, length us, event | category | flops | bytes accessed | tf_op | source)
XLA Modules:
  0.0 84.8 jit_solution(7087091370600575141)
XLA Ops:
  0.0 0.0 copy-start.2
  0.0 3.2 %collective-permute-start = (bf16[32,1024]{1,0:T(8,128)(2,1)}, bf16[32,1024]{1,0:T(8,128)(2,1)S(1)}, u32[]{:S(2)}, u32[]{:S(2)}) collective-permute-start(bf16[32,1024]{1,0:T(8,128)(2,1)} %bitcast.30), channel_id=1, source_target_pairs={{0,2},{1,3},{2,0},{3,1},{4,6},{5,7},{6,4},{7,5},{8,10},{9,11},{10,... | collective-permute-start | bytes 196616 | tf_op jit(solution)/shard_map/ppermute | solution.py:219
  3.2 0.8 fusion.7
  4.0 1.0 %broadcast_in_dim.7 = bf16[2,8,48,512]{3,2,1,0:T(8,128)(2,1)} broadcast(bf16[2,48,512]{2,1,0:T(8,128)(2,1)S(1)} %pad_maximum_fusion.1), dimensions={0,2,3} | broadcast | bytes 884736 | tf_op jit(solution)/shard_map/broadcast_in_dim | solution.py:252
  5.0 0.0 copy-start.4
  5.0 0.0 copy-start.3
  5.0 8.8 %all-to-all-start = ((bf16[16,48,512]{2,1,0:T(8,128)(2,1)}), bf16[16,48,512]{2,1,0:T(8,128)(2,1)S(1)}, u32[]{:S(2)}, u32[]{:S(2)}) async-start(bf16[16,48,512]{2,1,0:T(8,128)(2,1)} %bitcast.6), calls=%async_computation | async-start | bytes 1572864 | tf_op jit(solution)/shard_map/all_to_all | solution.py:253
  13.8 0.0 copy-done.2
  13.8 0.0 collective-permute-done
  13.9 1.3 %collective-permute-start.1 = (bf16[2,32,1024]{2,1,0:T(8,128)(2,1)S(1)}, bf16[2,32,1024]{2,1,0:T(8,128)(2,1)S(1)}, u32[]{:S(2)}, u32[]{:S(2)}) collective-permute-start(bf16[2,32,1024]{2,1,0:T(8,128)(2,1)S(1)} %pad_maximum_fusion), channel_id=1, source_target_pairs={{0,4},{1,5},{2,6},{3,7},{4,8},{5,9},{6,10},{7,11},{8,12},{9,13},{1... | collective-permute-start | bytes 393224 | tf_op jit(solution)/shard_map/ppermute | solution.py:219
  15.1 0.8 collective-permute-start.2
  15.9 1.1 %collective-permute-start.3 = (bf16[2,32,1024]{2,1,0:T(8,128)(2,1)S(1)}, bf16[2,32,1024]{2,1,0:T(8,128)(2,1)S(1)}, u32[]{:S(2)}, u32[]{:S(2)}) collective-permute-start(bf16[2,32,1024]{2,1,0:T(8,128)(2,1)S(1)} %pad_maximum_fusion), channel_id=1, source_target_pairs={{0,12},{1,13},{2,14},{3,15},{4,0},{5,1},{6,2},{7,3},{8,4},{9,5},{1... | collective-permute-start | bytes 393224 | tf_op jit(solution)/shard_map/ppermute | solution.py:219
  17.1 2.8 %collective-permute-done.1 = bf16[2,32,1024]{2,1,0:T(8,128)(2,1)S(1)} collective-permute-done((bf16[2,32,1024]{2,1,0:T(8,128)(2,1)S(1)}, bf16[2,32,1024]{2,1,0:T(8,128)(2,1)S(1)}, u32[]{:S(2)}, u32[]{:S(2)}) %collective-permute-start.1) | collective-permute-done | bytes 131104 | tf_op jit(solution)/shard_map/ppermute | solution.py:219
  19.9 1.9 %collective-permute-done.2 = bf16[2,32,1024]{2,1,0:T(8,128)(2,1)S(1)} collective-permute-done((bf16[2,32,1024]{2,1,0:T(8,128)(2,1)S(1)}, bf16[2,32,1024]{2,1,0:T(8,128)(2,1)S(1)}, u32[]{:S(2)}, u32[]{:S(2)}) %collective-permute-start.2) | collective-permute-done | bytes 131104 | tf_op jit(solution)/shard_map/ppermute | solution.py:219
  21.7 1.5 %collective-permute-done.3 = bf16[2,32,1024]{2,1,0:T(8,128)(2,1)S(1)} collective-permute-done((bf16[2,32,1024]{2,1,0:T(8,128)(2,1)S(1)}, bf16[2,32,1024]{2,1,0:T(8,128)(2,1)S(1)}, u32[]{:S(2)}, u32[]{:S(2)}) %collective-permute-start.3) | collective-permute-done | bytes 131104 | tf_op jit(solution)/shard_map/ppermute | solution.py:219
  23.3 0.1 collective-permute-start.4
  23.4 0.0 copy-done.4
  23.4 0.1 copy.13.inv.refs_2_
  23.5 0.0 copy-done.3
  23.5 0.1 copy.10
  23.6 0.1 reshape.26.list_ref.refs_1_
  24.3 1.0 %collective-permute-done.4.far = bf16[8,32,1024]{2,1,0:T(8,128)(2,1)S(1)} collective-permute-done((bf16[8,32,1024]{2,1,0:T(8,128)(2,1)S(1)}, bf16[8,32,1024]{2,1,0:T(8,128)(2,1)S(1)}, u32[]{:S(2)}, u32[]{:S(2)}) %collective-permute-start.4) | collective-permute-done | bytes 524320 | tf_op jit(solution)/shard_map/ppermute | solution.py:219
  25.3 1.0 %prepare_rows.1 = (bf16[6,1024,48]{2,1,0:T(8,128)(2,1)S(1)}, bf16[6,48,1024]{2,1,0:T(8,128)(2,1)S(1)}) custom-call(s32[1]{0:T(128)} %bitcast.27.live_ref, s32[12]{0:T(128)S(1)} %reshape.26.list_ref.refs_1_, f32[32,1]{1,0:T(8,128)S(1)} %copy.13.inv.refs_2_, bf16[8,32,1024]{2,1,0:T(8,128)(2,1)S(1)} %constant_dynamic-update-slice_fusion.near, ...), custom_call_target="tpu_custom_call" | custom-call | flops 2000000000 | bytes 1000000 | tf_op jit(solution)/shard_map/prepare_rows/pallas_call | solution.py:175
  26.3 0.0 copy-start
  26.3 0.8 copy-done
  27.1 7.4 %all-to-all-done.refs_5_ = bf16[16,48,512]{2,1,0:T(8,128)(2,1)S(1)} async-done(((bf16[16,48,512]{2,1,0:T(8,128)(2,1)}), bf16[16,48,512]{2,1,0:T(8,128)(2,1)S(1)}, u32[]{:S(2)}, u32[]{:S(2)}) %all-to-all-start) | async-done | bytes 786464 | tf_op jit(solution)/shard_map/all_to_all | solution.py:253
  34.5 1.0 %collective-permute-start.5 = (bf16[16,16,512]{2,1,0:T(8,128)(2,1)S(1)}, bf16[16,16,512]{2,1,0:T(8,128)(2,1)S(1)}, u32[]{:S(2)}, u32[]{:S(2)}) collective-permute-start(bf16[16,16,512]{2,1,0:T(8,128)(2,1)S(1)} %slice.47), channel_id=1, source_target_pairs={{0,128},{16,144},{32,160},{48,176},{64,192},{80,208},{96,224},{112... | collective-permute-start | bytes 786440 | tf_op jit(solution)/shard_map/ppermute | solution.py:245
  35.6 0.0 copy-start.1
  35.6 1.1 %copy-done.1 = bf16[6,48,1024]{2,1,0:T(8,128)(2,1)S(1)} copy-done((bf16[6,48,1024]{2,1,0:T(8,128)(2,1)S(1)}, bf16[6,48,1024]{2,1,0:T(8,128)(2,1)}, u32[]{:S(2)}) %copy-start.1) | copy-done | bytes 589848
  36.6 4.2 %first_half.1 = (f32[16,32,1024]{2,1,0:T(8,128)S(1)}, f32[16,16,512]{2,1,0:T(8,128)S(1)}, bf16[16,16,512]{2,1,0:T(8,128)(2,1)S(1)}) custom-call(s32[1]{0:T(128)} %bitcast.28.refs_0_, s32[12]{0:T(128)S(1)} %reshape.26.list_ref.refs_1_, f32[32,1]{1,0:T(8,128)S(1)} %copy.13.inv.refs_2_, bf16[6,1024,48]{2,1,0:T(8,128)(2,1)S(1)} %get-tuple-element.13.refs_3_, ...), custom_call_target="tpu_custom_call" | custom-call | flops 10000000000 | bytes 10000000 | tf_op jit(solution)/shard_map/first_half/pallas_call | solution.py:206
  40.8 2.2 %collective-permute-start.6 = (bf16[16,16,512]{2,1,0:T(8,128)(2,1)S(1)}, bf16[16,16,512]{2,1,0:T(8,128)(2,1)S(1)}, u32[]{:S(2)}, u32[]{:S(2)}) collective-permute-start(bf16[16,16,512]{2,1,0:T(8,128)(2,1)S(1)} %get-tuple-element.18), channel_id=1, source_target_pairs={{0,128},{16,144},{32,160},{48,176},{64,192},{80,208},{96,224},{112... | collective-permute-start | bytes 786440 | tf_op jit(solution)/shard_map/ppermute | solution.py:245
  43.0 0.0 collective-permute-done.5.refs_6_
  43.0 5.4 %second_half.1 = (bf16[8,32,1024]{2,1,0:T(8,128)(2,1)S(1)}, bf16[8,32,1024]{2,1,0:T(8,128)(2,1)S(1)}, bf16[16,48,512]{2,1,0:T(8,128)(2,1)}) custom-call(s32[1]{0:T(128)} %bitcast.29.refs_0_, s32[12]{0:T(128)S(1)} %reshape.26.list_ref.refs_1_, f32[32,1]{1,0:T(8,128)S(1)} %copy.13.inv.refs_2_, bf16[6,1024,48]{2,1,0:T(8,128)(2,1)S(1)} %get-tuple-element.13.refs_3_, ...), custom_call_target="tpu_custom_call" | custom-call | flops 10000000000 | bytes 10000000 | tf_op jit(solution)/shard_map/second_half/pallas_call | solution.py:206
  48.5 3.1 %collective-permute-start.7 = (bf16[8,32,1024]{2,1,0:T(8,128)(2,1)S(1)}, bf16[8,32,1024]{2,1,0:T(8,128)(2,1)S(1)}, u32[]{:S(2)}, u32[]{:S(2)}) collective-permute-start(bf16[8,32,1024]{2,1,0:T(8,128)(2,1)S(1)} %get-tuple-element.20), channel_id=1, source_target_pairs={{0,1},{1,0},{2,3},{3,2},{4,5},{5,4},{6,7},{7,6},{8,9},{9,8},{10,11... | collective-permute-start | bytes 1572872 | tf_op jit(solution)/shard_map/ppermute | solution.py:219
  51.6 0.0 collective-permute-done.6
  51.6 0.8 fusion
  52.4 9.0 %all-to-all-start.1 = ((bf16[16,48,512]{2,1,0:T(8,128)(2,1)}), bf16[16,48,512]{2,1,0:T(8,128)(2,1)S(1)}, u32[]{:S(2)}, u32[]{:S(2)}) async-start(bf16[16,48,512]{2,1,0:T(8,128)(2,1)} %fusion), calls=%async_computation.1 | async-start | bytes 1572864 | tf_op jit(solution)/shard_map/all_to_all | solution.py:257
  61.4 0.0 collective-permute-done.7
  61.4 0.2 add_convert_fusion
  61.6 0.1 collective-permute-start.10
  61.7 2.0 %collective-permute-start.8 = (bf16[2,32,1024]{2,1,0:T(8,128)(2,1)S(1)}, bf16[2,32,1024]{2,1,0:T(8,128)(2,1)S(1)}, u32[]{:S(2)}, u32[]{:S(2)}) collective-permute-start(bf16[2,32,1024]{2,1,0:T(8,128)(2,1)S(1)} %get-tuple-element.21), channel_id=1, source_target_pairs={{0,12},{1,13},{2,14},{3,15},{4,0},{5,1},{6,2},{7,3},{8,4},{9,5},{1... | collective-permute-start | bytes 393224 | tf_op jit(solution)/shard_map/ppermute | solution.py:219
  63.7 0.7 collective-permute-start.9
  64.4 2.9 %collective-permute-done.10 = bf16[2,32,1024]{2,1,0:T(8,128)(2,1)S(1)} collective-permute-done((bf16[2,32,1024]{2,1,0:T(8,128)(2,1)S(1)}, bf16[2,32,1024]{2,1,0:T(8,128)(2,1)S(1)}, u32[]{:S(2)}, u32[]{:S(2)}) %collective-permute-start.10) | collective-permute-done | bytes 131104 | tf_op jit(solution)/shard_map/ppermute | solution.py:219
  67.3 0.8 collective-permute-done.8
  68.1 2.2 %collective-permute-done.9 = bf16[2,32,1024]{2,1,0:T(8,128)(2,1)S(1)} collective-permute-done((bf16[2,32,1024]{2,1,0:T(8,128)(2,1)S(1)}, bf16[2,32,1024]{2,1,0:T(8,128)(2,1)S(1)}, u32[]{:S(2)}, u32[]{:S(2)}) %collective-permute-start.9) | collective-permute-done | bytes 131104 | tf_op jit(solution)/shard_map/ppermute | solution.py:219
  70.3 0.1 convert_add_fusion
  70.4 0.7 collective-permute-start.11
  71.1 12.6 %all-to-all-done.1 = bf16[16,48,512]{2,1,0:T(8,128)(2,1)S(1)} async-done(((bf16[16,48,512]{2,1,0:T(8,128)(2,1)}), bf16[16,48,512]{2,1,0:T(8,128)(2,1)S(1)}, u32[]{:S(2)}, u32[]{:S(2)}) %all-to-all-start.1) | async-done | bytes 786464 | tf_op jit(solution)/shard_map/all_to_all | solution.py:257
  83.7 0.2 convert_element_type.39
  83.9 0.1 slice_reduce_fusion
  84.1 0.0 collective-permute-done.11
  84.1 0.7 fusion.4
  (13 shorter events, 0.2 us)
Async XLA Ops:
  0.0 13.8 %copy-start.2 = (bf16[1,1,32,1024]{3,2,1,0:T(8,128)(2,1)S(1)}, bf16[1,1,32,1024]{3,2,1,0:T(8,128)(2,1)}, u32[]{:S(2)}) copy-start(bf16[1,1,32,1024]{3,2,1,0:T(8,128)(2,1)} %param.5) | copy-start | bytes 196612
  0.0 13.8 %collective-permute-start = (bf16[32,1024]{1,0:T(8,128)(2,1)}, bf16[32,1024]{1,0:T(8,128)(2,1)S(1)}, u32[]{:S(2)}, u32[]{:S(2)}) collective-permute-start(bf16[32,1024]{1,0:T(8,128)(2,1)} %bitcast.30), channel_id=1, source_target_pairs={{0,2},{1,3},{2,0},{3,1},{4,6},{5,7},{6,4},{7,5},{8,10},{9,11},{10,... | collective-permute-start | bytes 196616 | tf_op jit(solution)/shard_map/ppermute | solution.py:219
  5.0 18.4 %copy-start.4 = (f32[32]{0:T(128)S(1)}, f32[32]{0:T(128)}, u32[]{:S(2)}) copy-start(f32[32]{0:T(128)} %param.6) | copy-start | bytes 388
  5.0 18.5 %copy-start.3 = (s32[1,1,6,2]{2,3,1,0:T(2,128)S(1)}, s32[1,1,6,2]{2,3,1,0:T(2,128)}, u32[]{:S(2)}) copy-start(s32[1,1,6,2]{2,3,1,0:T(2,128)} %param.8) | copy-start | bytes 148
  5.0 29.5 %all-to-all-start = ((bf16[16,48,512]{2,1,0:T(8,128)(2,1)}), bf16[16,48,512]{2,1,0:T(8,128)(2,1)S(1)}, u32[]{:S(2)}, u32[]{:S(2)}) async-start(bf16[16,48,512]{2,1,0:T(8,128)(2,1)} %bitcast.6), calls=%async_computation | async-start | bytes 1572864 | tf_op jit(solution)/shard_map/all_to_all | solution.py:253
  13.9 6.0 %collective-permute-start.1 = (bf16[2,32,1024]{2,1,0:T(8,128)(2,1)S(1)}, bf16[2,32,1024]{2,1,0:T(8,128)(2,1)S(1)}, u32[]{:S(2)}, u32[]{:S(2)}) collective-permute-start(bf16[2,32,1024]{2,1,0:T(8,128)(2,1)S(1)} %pad_maximum_fusion), channel_id=1, source_target_pairs={{0,4},{1,5},{2,6},{3,7},{4,8},{5,9},{6,10},{7,11},{8,12},{9,13},{1... | collective-permute-start | bytes 393224 | tf_op jit(solution)/shard_map/ppermute | solution.py:219
  15.1 6.6 %collective-permute-start.2 = (bf16[2,32,1024]{2,1,0:T(8,128)(2,1)S(1)}, bf16[2,32,1024]{2,1,0:T(8,128)(2,1)S(1)}, u32[]{:S(2)}, u32[]{:S(2)}) collective-permute-start(bf16[2,32,1024]{2,1,0:T(8,128)(2,1)S(1)} %pad_maximum_fusion), channel_id=1, source_target_pairs={{0,8},{1,9},{2,10},{3,11},{4,12},{5,13},{6,14},{7,15},{8,0},{9,1},... | collective-permute-start | bytes 393224 | tf_op jit(solution)/shard_map/ppermute | solution.py:219
  15.9 7.3 %collective-permute-start.3 = (bf16[2,32,1024]{2,1,0:T(8,128)(2,1)S(1)}, bf16[2,32,1024]{2,1,0:T(8,128)(2,1)S(1)}, u32[]{:S(2)}, u32[]{:S(2)}) collective-permute-start(bf16[2,32,1024]{2,1,0:T(8,128)(2,1)S(1)} %pad_maximum_fusion), channel_id=1, source_target_pairs={{0,12},{1,13},{2,14},{3,15},{4,0},{5,1},{6,2},{7,3},{8,4},{9,5},{1... | collective-permute-start | bytes 393224 | tf_op jit(solution)/shard_map/ppermute | solution.py:219
  23.3 2.0 %collective-permute-start.4 = (bf16[8,32,1024]{2,1,0:T(8,128)(2,1)S(1)}, bf16[8,32,1024]{2,1,0:T(8,128)(2,1)S(1)}, u32[]{:S(2)}, u32[]{:S(2)}) collective-permute-start(bf16[8,32,1024]{2,1,0:T(8,128)(2,1)S(1)} %constant_dynamic-update-slice_fusion.near), channel_id=1, source_target_pairs={{0,1},{1,0},{2,3},{3,2},{4,5},{5,4},{6,7},{7,6},{8,9},{9,8},{10,11... | collective-permute-start | bytes 1572872 | tf_op jit(solution)/shard_map/ppermute | solution.py:219
  26.3 0.8 copy-start
  34.5 8.5 %collective-permute-start.5 = (bf16[16,16,512]{2,1,0:T(8,128)(2,1)S(1)}, bf16[16,16,512]{2,1,0:T(8,128)(2,1)S(1)}, u32[]{:S(2)}, u32[]{:S(2)}) collective-permute-start(bf16[16,16,512]{2,1,0:T(8,128)(2,1)S(1)} %slice.47), channel_id=1, source_target_pairs={{0,128},{16,144},{32,160},{48,176},{64,192},{80,208},{96,224},{112... | collective-permute-start | bytes 786440 | tf_op jit(solution)/shard_map/ppermute | solution.py:245
  35.6 1.1 %copy-start.1 = (bf16[6,48,1024]{2,1,0:T(8,128)(2,1)S(1)}, bf16[6,48,1024]{2,1,0:T(8,128)(2,1)}, u32[]{:S(2)}) copy-start(bf16[6,48,1024]{2,1,0:T(8,128)(2,1)} %copy-done) | copy-start | bytes 1769476
  40.8 10.7 %collective-permute-start.6 = (bf16[16,16,512]{2,1,0:T(8,128)(2,1)S(1)}, bf16[16,16,512]{2,1,0:T(8,128)(2,1)S(1)}, u32[]{:S(2)}, u32[]{:S(2)}) collective-permute-start(bf16[16,16,512]{2,1,0:T(8,128)(2,1)S(1)} %get-tuple-element.18), channel_id=1, source_target_pairs={{0,128},{16,144},{32,160},{48,176},{64,192},{80,208},{96,224},{112... | collective-permute-start | bytes 786440 | tf_op jit(solution)/shard_map/ppermute | solution.py:245
  48.5 12.9 %collective-permute-start.7 = (bf16[8,32,1024]{2,1,0:T(8,128)(2,1)S(1)}, bf16[8,32,1024]{2,1,0:T(8,128)(2,1)S(1)}, u32[]{:S(2)}, u32[]{:S(2)}) collective-permute-start(bf16[8,32,1024]{2,1,0:T(8,128)(2,1)S(1)} %get-tuple-element.20), channel_id=1, source_target_pairs={{0,1},{1,0},{2,3},{3,2},{4,5},{5,4},{6,7},{7,6},{8,9},{9,8},{10,11... | collective-permute-start | bytes 1572872 | tf_op jit(solution)/shard_map/ppermute | solution.py:219
  52.4 31.3 %all-to-all-start.1 = ((bf16[16,48,512]{2,1,0:T(8,128)(2,1)}), bf16[16,48,512]{2,1,0:T(8,128)(2,1)S(1)}, u32[]{:S(2)}, u32[]{:S(2)}) async-start(bf16[16,48,512]{2,1,0:T(8,128)(2,1)} %fusion), calls=%async_computation.1 | async-start | bytes 1572864 | tf_op jit(solution)/shard_map/all_to_all | solution.py:257
  61.6 5.7 %collective-permute-start.10 = (bf16[2,32,1024]{2,1,0:T(8,128)(2,1)S(1)}, bf16[2,32,1024]{2,1,0:T(8,128)(2,1)S(1)}, u32[]{:S(2)}, u32[]{:S(2)}) collective-permute-start(bf16[2,32,1024]{2,1,0:T(8,128)(2,1)S(1)} %get-tuple-element.22), channel_id=1, source_target_pairs={{0,4},{1,5},{2,6},{3,7},{4,8},{5,9},{6,10},{7,11},{8,12},{9,13},{1... | collective-permute-start | bytes 393224 | tf_op jit(solution)/shard_map/ppermute | solution.py:219
  61.7 6.4 %collective-permute-start.8 = (bf16[2,32,1024]{2,1,0:T(8,128)(2,1)S(1)}, bf16[2,32,1024]{2,1,0:T(8,128)(2,1)S(1)}, u32[]{:S(2)}, u32[]{:S(2)}) collective-permute-start(bf16[2,32,1024]{2,1,0:T(8,128)(2,1)S(1)} %get-tuple-element.21), channel_id=1, source_target_pairs={{0,12},{1,13},{2,14},{3,15},{4,0},{5,1},{6,2},{7,3},{8,4},{9,5},{1... | collective-permute-start | bytes 393224 | tf_op jit(solution)/shard_map/ppermute | solution.py:219
  63.7 6.6 %collective-permute-start.9 = (bf16[2,32,1024]{2,1,0:T(8,128)(2,1)S(1)}, bf16[2,32,1024]{2,1,0:T(8,128)(2,1)S(1)}, u32[]{:S(2)}, u32[]{:S(2)}) collective-permute-start(bf16[2,32,1024]{2,1,0:T(8,128)(2,1)S(1)} %get-tuple-element.23), channel_id=1, source_target_pairs={{0,8},{1,9},{2,10},{3,11},{4,12},{5,13},{6,14},{7,15},{8,0},{9,1},... | collective-permute-start | bytes 393224 | tf_op jit(solution)/shard_map/ppermute | solution.py:219
  70.4 13.7 %collective-permute-start.11 = (bf16[32,1024]{1,0:T(8,128)(2,1)S(1)}, bf16[32,1024]{1,0:T(8,128)(2,1)S(1)}, u32[]{:S(2)}, u32[]{:S(2)}) collective-permute-start(bf16[32,1024]{1,0:T(8,128)(2,1)S(1)} %fusion.5), channel_id=1, source_target_pairs={{0,2},{1,3},{2,0},{3,1},{4,6},{5,7},{6,4},{7,5},{8,10},{9,11},{10,... | collective-permute-start | bytes 196616 | tf_op jit(solution)/shard_map/ppermute | solution.py:219

commit v4 on v3

--- a/solution.py
+++ b/solution.py
@@ -85,7 +85,7 @@
     def _():
         fetch(1).start()
 
-    racc[...] = jnp.zeros(racc.shape, f32)
+    racc[...] = carry[...] if second else jnp.zeros(racc.shape, f32)
     cacc[...] = jnp.zeros(cacc.shape, f32)
     zj1[1] = jnp.zeros((K, TJ), bf16)
     cb[NS - 1] = jnp.zeros((SI, TJ), bf16)
@@ -158,10 +158,9 @@
         rt = part if rt is None else rt + part
     finish(NS - 1, last, ib, scale, rt)
     if second:
-        rout[...] = (racc[:HALF] + carry[:HALF]).astype(bf16)
-        rout2[...] = (racc[HALF:] + carry[HALF:]).astype(bf16)
+        rout[...] = racc[:HALF].astype(bf16)
+        rout2[...] = racc[HALF:].astype(bf16)
         cout[:, :F] = cacc[...].astype(bf16)
-        cout[:, F:] = jnp.zeros((N, FH, TJ), bf16)
     else:
         keep[...] = cacc[:, pl.ds(mine, FH)]
         send[...] = cacc[:, pl.ds(other, FH)].astype(bf16)
@@ -245,12 +244,33 @@
     return lax.ppermute(x, "row", [(i, i ^ HALF) for i in range(N)])
 
 
+def spread(block, copies):
+    for d in range(N):
+        part = d // HALF * FH
+        copies[d, :F] = block[:, :TJ]
+        copies[d, F:] = block[part : part + FH, TJ:]
+
+
+def echo(block, copies, same):
+    same[...] = block[...]
+
+
 def gather_row(block):
-    whole = jnp.broadcast_to(block[None, :, :TJ], (2, F, TJ))
-    part = block[:, TJ:].reshape(2, FH, TJ)
-    copies = jnp.concatenate([whole, part], axis=1)
-    copies = jnp.broadcast_to(copies[:, None], (2, HALF, F + FH, TJ)).reshape(N, F + FH, TJ)
-    return lax.all_to_all(copies, "row", 0, 0, tiled=True)
+    copies = pl.pallas_call(
+        spread,
+        out_shape=jax.ShapeDtypeStruct((N, F + FH, TJ), bf16),
+        in_specs=[VMEM],
+        out_specs=VMEM,
+        name="spread",
+    )(block)
+    same = pl.pallas_call(
+        echo,
+        out_shape=jax.ShapeDtypeStruct((F, TB), bf16),
+        in_specs=[VMEM, pl.BlockSpec(memory_space=pl.ANY)],
+        out_specs=VMEM,
+        name="echo",
+    )(block, copies)
+    return lax.all_to_all(copies, "row", 0, 0, tiled=True), same
 
 
 def scatter_row(parts):
@@ -263,7 +283,7 @@
 def body(features, inv_scales, inverse_tiles, tile_list, live_count):
     block = features[0, 0]
     live, places, inv = live_count.reshape(1), tile_list.reshape(2 * S), inv_scales.reshape(F, 1)
-    cols = gather_row(block)
+    cols, block = gather_row(block)
     near, far = gather_col(block)
     lhs, zi1 = prepare_pass(live, places, inv, near, far)
     swapped = swap_y(cols[:, F:])

time: 84.8 us -> 88 us (1.038)
  the two profiles are of different devices: /device:TPU:4 before, /device:TPU:16 now
where the time goes in v4:
time: 88 us; the launch traced here: 88.1 us
  starting transfers between devices  39.2 us (45%)
  waiting for transfers between devices  28.4 us (32%)
  Pallas kernels  13.5 us (15%)
  local copies, waits for them, and re-layouts  3.11 us (4%)
  other arithmetic  2.97 us (3%)
    ppermute x10, waiting for transfers between devices, move(): return lax.ppermute(x, 'col', [(i, to(i)) for i in range(N)])  16.4 us
    all_to_all x1, starting transfers between devices, scatter_row(): got = lax.all_to_all(parts, 'row', 0, 0, tiled=True).astype(f32)  12.7 us
    all_to_all x1, waiting for transfers between devices, scatter_row(): got = lax.all_to_all(parts, 'row', 0, 0, tiled=True).astype(f32)  12 us
    ppermute x10, starting transfers between devices, move(): return lax.ppermute(x, 'col', [(i, to(i)) for i in range(N)])  9.95 us
    all_to_all x1, starting transfers between devices, gather_row(): return (lax.all_to_all(copies, 'row', 0, 0, tiled=True), same)  9.42 us
    pallas_call x2, Pallas kernels, tile_pass(): pl.pallas_call(run, out_shape=outs, in_specs=[SMEM] * 2 + [VMEM] * (len(a...  9.23 us
    ppermute x2, starting transfers between devices, swap_y(): return lax.ppermute(x, 'row', [(i, i ^ HALF) for i in range(N)])  7.19 us
    unnamed x13, local copies, waits for them, and re-layouts  2.88 us
  transfers between devices with their start and end apart: 14, of which 9 were waited for; matrix products, arithmetic and copies ran while one was open for 4% of the time, Pallas kernels for 13%

profile of v4, /device:TPU:16, one launch (start us, length us, event | category | flops | bytes accessed | tf_op | source)
XLA Modules:
  0.0 88.1 jit_solution(8726816062029129877)
XLA Ops:
  0.0 1.8 %spread.1.copies = bf16[16,48,512]{2,1,0:T(8,128)(2,1)} custom-call(bf16[32,1024]{1,0:T(8,128)(2,1)} %bitcast.29), custom_call_target="tpu_custom_call" | custom-call | tf_op jit(solution)/shard_map/spread/pallas_call | solution.py:259
  1.8 0.0 copy-start.3
  1.8 0.0 copy-start.2
  1.8 9.4 %all-to-all-start = ((bf16[16,48,512]{2,1,0:T(8,128)(2,1)}), bf16[16,48,512]{2,1,0:T(8,128)(2,1)S(1)}, u32[]{:S(2)}, u32[]{:S(2)}) async-start(bf16[16,48,512]{2,1,0:T(8,128)(2,1)} %spread.1.copies), calls=%async_computation | async-start | bytes 1572864 | tf_op jit(solution)/shard_map/all_to_all | solution.py:273
  11.2 1.5 %echo.1 = bf16[32,1024]{1,0:T(8,128)(2,1)} custom-call(bf16[32,1024]{1,0:T(8,128)(2,1)} %bitcast.30, bf16[16,48,512]{2,1,0:T(8,128)(2,1)} %spread.1.copies), custom_call_target="tpu_custom_call" | custom-call | tf_op jit(solution)/shard_map/echo/pallas_call | solution.py:266
  12.7 0.6 collective-permute-start
  13.3 0.9 constant_dynamic-update-slice_fusion.4
  14.2 5.4 %collective-permute-done = bf16[32,1024]{1,0:T(8,128)(2,1)S(1)} collective-permute-done((bf16[32,1024]{1,0:T(8,128)(2,1)}, bf16[32,1024]{1,0:T(8,128)(2,1)S(1)}, u32[]{:S(2)}, u32[]{:S(2)}) %collective-permute-start) | collective-permute-done | bytes 65568 | tf_op jit(solution)/shard_map/ppermute | solution.py:218
  19.6 0.9 pad_maximum_fusion
  20.4 1.6 %collective-permute-start.1 = (bf16[2,32,1024]{2,1,0:T(8,128)(2,1)S(1)}, bf16[2,32,1024]{2,1,0:T(8,128)(2,1)S(1)}, u32[]{:S(2)}, u32[]{:S(2)}) collective-permute-start(bf16[2,32,1024]{2,1,0:T(8,128)(2,1)S(1)} %pad_maximum_fusion), channel_id=1, source_target_pairs={{0,4},{1,5},{2,6},{3,7},{4,8},{5,9},{6,10},{7,11},{8,12},{9,13},{1... | collective-permute-start | bytes 393224 | tf_op jit(solution)/shard_map/ppermute | solution.py:218
  22.0 2.7 %collective-permute-start.2 = (bf16[2,32,1024]{2,1,0:T(8,128)(2,1)S(1)}, bf16[2,32,1024]{2,1,0:T(8,128)(2,1)S(1)}, u32[]{:S(2)}, u32[]{:S(2)}) collective-permute-start(bf16[2,32,1024]{2,1,0:T(8,128)(2,1)S(1)} %pad_maximum_fusion), channel_id=1, source_target_pairs={{0,8},{1,9},{2,10},{3,11},{4,12},{5,13},{6,14},{7,15},{8,0},{9,1},... | collective-permute-start | bytes 393224 | tf_op jit(solution)/shard_map/ppermute | solution.py:218
  24.7 1.4 %collective-permute-start.3 = (bf16[2,32,1024]{2,1,0:T(8,128)(2,1)S(1)}, bf16[2,32,1024]{2,1,0:T(8,128)(2,1)S(1)}, u32[]{:S(2)}, u32[]{:S(2)}) collective-permute-start(bf16[2,32,1024]{2,1,0:T(8,128)(2,1)S(1)} %pad_maximum_fusion), channel_id=1, source_target_pairs={{0,12},{1,13},{2,14},{3,15},{4,0},{5,1},{6,2},{7,3},{8,4},{9,5},{1... | collective-permute-start | bytes 393224 | tf_op jit(solution)/shard_map/ppermute | solution.py:218
  26.1 0.9 %collective-permute-done.1 = bf16[2,32,1024]{2,1,0:T(8,128)(2,1)S(1)} collective-permute-done((bf16[2,32,1024]{2,1,0:T(8,128)(2,1)S(1)}, bf16[2,32,1024]{2,1,0:T(8,128)(2,1)S(1)}, u32[]{:S(2)}, u32[]{:S(2)}) %collective-permute-start.1) | collective-permute-done | bytes 131104 | tf_op jit(solution)/shard_map/ppermute | solution.py:218
  27.1 2.0 %collective-permute-done.2 = bf16[2,32,1024]{2,1,0:T(8,128)(2,1)S(1)} collective-permute-done((bf16[2,32,1024]{2,1,0:T(8,128)(2,1)S(1)}, bf16[2,32,1024]{2,1,0:T(8,128)(2,1)S(1)}, u32[]{:S(2)}, u32[]{:S(2)}) %collective-permute-start.2) | collective-permute-done | bytes 131104 | tf_op jit(solution)/shard_map/ppermute | solution.py:218
  29.1 0.6 collective-permute-done.3
  29.7 0.1 collective-permute-start.4
  29.8 0.0 copy-done.3
  29.8 0.1 copy.13.inv.refs_2_
  29.9 0.0 copy-done.2
  29.9 0.1 copy.10
  30.0 0.1 reshape.18.list_ref.refs_1_
  30.7 1.0 %collective-permute-done.4.far = bf16[8,32,1024]{2,1,0:T(8,128)(2,1)S(1)} collective-permute-done((bf16[8,32,1024]{2,1,0:T(8,128)(2,1)S(1)}, bf16[8,32,1024]{2,1,0:T(8,128)(2,1)S(1)}, u32[]{:S(2)}, u32[]{:S(2)}) %collective-permute-start.4) | collective-permute-done | bytes 524320 | tf_op jit(solution)/shard_map/ppermute | solution.py:218
  31.7 1.0 %prepare_rows.1 = (bf16[6,1024,48]{2,1,0:T(8,128)(2,1)S(1)}, bf16[6,48,1024]{2,1,0:T(8,128)(2,1)S(1)}) custom-call(s32[1]{0:T(128)} %bitcast.25.live_ref, s32[12]{0:T(128)S(1)} %reshape.18.list_ref.refs_1_, f32[32,1]{1,0:T(8,128)S(1)} %copy.13.inv.refs_2_, bf16[8,32,1024]{2,1,0:T(8,128)(2,1)S(1)} %constant_dynamic-update-slice_fusion.near, ...), custom_call_target="tpu_custom_call" | custom-call | flops 2000000000 | bytes 1000000 | tf_op jit(solution)/shard_map/prepare_rows/pallas_call | solution.py:174
  32.7 0.0 copy-start
  32.7 0.8 copy-done
  33.5 0.0 all-to-all-done.refs_5_
  33.5 3.0 %collective-permute-start.5 = (bf16[16,16,512]{2,1,0:T(8,128)(2,1)S(1)}, bf16[16,16,512]{2,1,0:T(8,128)(2,1)S(1)}, u32[]{:S(2)}, u32[]{:S(2)}) collective-permute-start(bf16[16,16,512]{2,1,0:T(8,128)(2,1)S(1)} %slice.37), channel_id=1, source_target_pairs={{0,128},{16,144},{32,160},{48,176},{64,192},{80,208},{96,224},{112... | collective-permute-start | bytes 786440 | tf_op jit(solution)/shard_map/ppermute | solution.py:244
  36.6 0.0 copy-start.1
  36.6 1.1 %copy-done.1 = bf16[6,48,1024]{2,1,0:T(8,128)(2,1)S(1)} copy-done((bf16[6,48,1024]{2,1,0:T(8,128)(2,1)S(1)}, bf16[6,48,1024]{2,1,0:T(8,128)(2,1)}, u32[]{:S(2)}) %copy-start.1) | copy-done | bytes 589848
  37.6 4.2 %first_half.1 = (f32[16,32,1024]{2,1,0:T(8,128)S(1)}, f32[16,16,512]{2,1,0:T(8,128)S(1)}, bf16[16,16,512]{2,1,0:T(8,128)(2,1)S(1)}) custom-call(s32[1]{0:T(128)} %bitcast.26.refs_0_, s32[12]{0:T(128)S(1)} %reshape.18.list_ref.refs_1_, f32[32,1]{1,0:T(8,128)S(1)} %copy.13.inv.refs_2_, bf16[6,1024,48]{2,1,0:T(8,128)(2,1)S(1)} %get-tuple-element.13.refs_3_, ...), custom_call_target="tpu_custom_call" | custom-call | flops 10000000000 | bytes 10000000 | tf_op jit(solution)/shard_map/first_half/pallas_call | solution.py:205
  41.8 4.2 %collective-permute-start.6 = (bf16[16,16,512]{2,1,0:T(8,128)(2,1)S(1)}, bf16[16,16,512]{2,1,0:T(8,128)(2,1)S(1)}, u32[]{:S(2)}, u32[]{:S(2)}) collective-permute-start(bf16[16,16,512]{2,1,0:T(8,128)(2,1)S(1)} %get-tuple-element.18), channel_id=1, source_target_pairs={{0,128},{16,144},{32,160},{48,176},{64,192},{80,208},{96,224},{112... | collective-permute-start | bytes 786440 | tf_op jit(solution)/shard_map/ppermute | solution.py:244
  46.0 0.0 collective-permute-done.5.refs_6_
  46.0 5.0 %second_half.1 = (bf16[8,32,1024]{2,1,0:T(8,128)(2,1)S(1)}, bf16[8,32,1024]{2,1,0:T(8,128)(2,1)S(1)}, bf16[16,48,512]{2,1,0:T(8,128)(2,1)}) custom-call(s32[1]{0:T(128)} %bitcast.27.refs_0_, s32[12]{0:T(128)S(1)} %reshape.18.list_ref.refs_1_, f32[32,1]{1,0:T(8,128)S(1)} %copy.13.inv.refs_2_, bf16[6,1024,48]{2,1,0:T(8,128)(2,1)S(1)} %get-tuple-element.13.refs_3_, ...), custom_call_target="tpu_custom_call" | custom-call | flops 10000000000 | bytes 10000000 | tf_op jit(solution)/shard_map/second_half/pallas_call | solution.py:205
  51.1 0.1 collective-permute-start.7
  51.2 0.0 collective-permute-done.6
  51.2 0.8 fusion
  52.0 12.7 %all-to-all-start.1 = ((bf16[16,48,512]{2,1,0:T(8,128)(2,1)}), bf16[16,48,512]{2,1,0:T(8,128)(2,1)S(1)}, u32[]{:S(2)}, u32[]{:S(2)}) async-start(bf16[16,48,512]{2,1,0:T(8,128)(2,1)} %fusion), calls=%async_computation.1 | async-start | bytes 1572864 | tf_op jit(solution)/shard_map/all_to_all | solution.py:277
  64.6 0.0 collective-permute-done.7
  64.7 0.2 add_convert_fusion
  64.9 0.1 collective-permute-start.10
  65.0 3.2 %collective-permute-start.8 = (bf16[2,32,1024]{2,1,0:T(8,128)(2,1)S(1)}, bf16[2,32,1024]{2,1,0:T(8,128)(2,1)S(1)}, u32[]{:S(2)}, u32[]{:S(2)}) collective-permute-start(bf16[2,32,1024]{2,1,0:T(8,128)(2,1)S(1)} %get-tuple-element.21), channel_id=1, source_target_pairs={{0,12},{1,13},{2,14},{3,15},{4,0},{5,1},{6,2},{7,3},{8,4},{9,5},{1... | collective-permute-start | bytes 393224 | tf_op jit(solution)/shard_map/ppermute | solution.py:218
  68.2 0.0 collective-permute-start.9
  68.2 3.6 %collective-permute-done.10 = bf16[2,32,1024]{2,1,0:T(8,128)(2,1)S(1)} collective-permute-done((bf16[2,32,1024]{2,1,0:T(8,128)(2,1)S(1)}, bf16[2,32,1024]{2,1,0:T(8,128)(2,1)S(1)}, u32[]{:S(2)}, u32[]{:S(2)}) %collective-permute-start.10) | collective-permute-done | bytes 131104 | tf_op jit(solution)/shard_map/ppermute | solution.py:218
  71.8 2.1 %collective-permute-done.8 = bf16[2,32,1024]{2,1,0:T(8,128)(2,1)S(1)} collective-permute-done((bf16[2,32,1024]{2,1,0:T(8,128)(2,1)S(1)}, bf16[2,32,1024]{2,1,0:T(8,128)(2,1)S(1)}, u32[]{:S(2)}, u32[]{:S(2)}) %collective-permute-start.8) | collective-permute-done | bytes 131104 | tf_op jit(solution)/shard_map/ppermute | solution.py:218
  73.9 0.9 %collective-permute-done.9 = bf16[2,32,1024]{2,1,0:T(8,128)(2,1)S(1)} collective-permute-done((bf16[2,32,1024]{2,1,0:T(8,128)(2,1)S(1)}, bf16[2,32,1024]{2,1,0:T(8,128)(2,1)S(1)}, u32[]{:S(2)}, u32[]{:S(2)}) %collective-permute-start.9) | collective-permute-done | bytes 131104 | tf_op jit(solution)/shard_map/ppermute | solution.py:218
  74.8 0.1 convert_add_fusion
  74.8 0.1 collective-permute-start.11
  75.0 12.0 %all-to-all-done.1 = bf16[16,48,512]{2,1,0:T(8,128)(2,1)S(1)} async-done(((bf16[16,48,512]{2,1,0:T(8,128)(2,1)}), bf16[16,48,512]{2,1,0:T(8,128)(2,1)S(1)}, u32[]{:S(2)}, u32[]{:S(2)}) %all-to-all-start.1) | async-done | bytes 786464 | tf_op jit(solution)/shard_map/all_to_all | solution.py:277
  87.0 0.2 convert_element_type.39
  87.2 0.1 slice_reduce_fusion
  87.3 0.0 collective-permute-done.11
  87.3 0.7 fusion.4
  (9 shorter events, 0.1 us)
Async XLA Ops:
  1.8 28.0 %copy-start.3 = (f32[32]{0:T(128)S(1)}, f32[32]{0:T(128)}, u32[]{:S(2)}) copy-start(f32[32]{0:T(128)} %param.6) | copy-start | bytes 388
  1.8 28.1 %copy-start.2 = (s32[1,1,6,2]{2,3,1,0:T(2,128)S(1)}, s32[1,1,6,2]{2,3,1,0:T(2,128)}, u32[]{:S(2)}) copy-start(s32[1,1,6,2]{2,3,1,0:T(2,128)} %param.8) | copy-start | bytes 148
  1.8 31.7 %all-to-all-start = ((bf16[16,48,512]{2,1,0:T(8,128)(2,1)}), bf16[16,48,512]{2,1,0:T(8,128)(2,1)S(1)}, u32[]{:S(2)}, u32[]{:S(2)}) async-start(bf16[16,48,512]{2,1,0:T(8,128)(2,1)} %spread.1.copies), calls=%async_computation | async-start | bytes 1572864 | tf_op jit(solution)/shard_map/all_to_all | solution.py:273
  12.7 6.9 %collective-permute-start = (bf16[32,1024]{1,0:T(8,128)(2,1)}, bf16[32,1024]{1,0:T(8,128)(2,1)S(1)}, u32[]{:S(2)}, u32[]{:S(2)}) collective-permute-start(bf16[32,1024]{1,0:T(8,128)(2,1)} %echo.1), channel_id=1, source_target_pairs={{0,2},{1,3},{2,0},{3,1},{4,6},{5,7},{6,4},{7,5},{8,10},{9,11},{10,... | collective-permute-start | bytes 196616 | tf_op jit(solution)/shard_map/ppermute | solution.py:218
  20.4 6.7 %collective-permute-start.1 = (bf16[2,32,1024]{2,1,0:T(8,128)(2,1)S(1)}, bf16[2,32,1024]{2,1,0:T(8,128)(2,1)S(1)}, u32[]{:S(2)}, u32[]{:S(2)}) collective-permute-start(bf16[2,32,1024]{2,1,0:T(8,128)(2,1)S(1)} %pad_maximum_fusion), channel_id=1, source_target_pairs={{0,4},{1,5},{2,6},{3,7},{4,8},{5,9},{6,10},{7,11},{8,12},{9,13},{1... | collective-permute-start | bytes 393224 | tf_op jit(solution)/shard_map/ppermute | solution.py:218
  22.0 7.1 %collective-permute-start.2 = (bf16[2,32,1024]{2,1,0:T(8,128)(2,1)S(1)}, bf16[2,32,1024]{2,1,0:T(8,128)(2,1)S(1)}, u32[]{:S(2)}, u32[]{:S(2)}) collective-permute-start(bf16[2,32,1024]{2,1,0:T(8,128)(2,1)S(1)} %pad_maximum_fusion), channel_id=1, source_target_pairs={{0,8},{1,9},{2,10},{3,11},{4,12},{5,13},{6,14},{7,15},{8,0},{9,1},... | collective-permute-start | bytes 393224 | tf_op jit(solution)/shard_map/ppermute | solution.py:218
  24.7 5.0 %collective-permute-start.3 = (bf16[2,32,1024]{2,1,0:T(8,128)(2,1)S(1)}, bf16[2,32,1024]{2,1,0:T(8,128)(2,1)S(1)}, u32[]{:S(2)}, u32[]{:S(2)}) collective-permute-start(bf16[2,32,1024]{2,1,0:T(8,128)(2,1)S(1)} %pad_maximum_fusion), channel_id=1, source_target_pairs={{0,12},{1,13},{2,14},{3,15},{4,0},{5,1},{6,2},{7,3},{8,4},{9,5},{1... | collective-permute-start | bytes 393224 | tf_op jit(solution)/shard_map/ppermute | solution.py:218
  29.7 2.0 %collective-permute-start.4 = (bf16[8,32,1024]{2,1,0:T(8,128)(2,1)S(1)}, bf16[8,32,1024]{2,1,0:T(8,128)(2,1)S(1)}, u32[]{:S(2)}, u32[]{:S(2)}) collective-permute-start(bf16[8,32,1024]{2,1,0:T(8,128)(2,1)S(1)} %constant_dynamic-update-slice_fusion.near), channel_id=1, source_target_pairs={{0,1},{1,0},{2,3},{3,2},{4,5},{5,4},{6,7},{7,6},{8,9},{9,8},{10,11... | collective-permute-start | bytes 1572872 | tf_op jit(solution)/shard_map/ppermute | solution.py:218
  32.7 0.8 copy-start
  33.5 12.5 %collective-permute-start.5 = (bf16[16,16,512]{2,1,0:T(8,128)(2,1)S(1)}, bf16[16,16,512]{2,1,0:T(8,128)(2,1)S(1)}, u32[]{:S(2)}, u32[]{:S(2)}) collective-permute-start(bf16[16,16,512]{2,1,0:T(8,128)(2,1)S(1)} %slice.37), channel_id=1, source_target_pairs={{0,128},{16,144},{32,160},{48,176},{64,192},{80,208},{96,224},{112... | collective-permute-start | bytes 786440 | tf_op jit(solution)/shard_map/ppermute | solution.py:244
  36.6 1.1 %copy-start.1 = (bf16[6,48,1024]{2,1,0:T(8,128)(2,1)S(1)}, bf16[6,48,1024]{2,1,0:T(8,128)(2,1)}, u32[]{:S(2)}) copy-start(bf16[6,48,1024]{2,1,0:T(8,128)(2,1)} %copy-done) | copy-start | bytes 1769476
  41.8 9.3 %collective-permute-start.6 = (bf16[16,16,512]{2,1,0:T(8,128)(2,1)S(1)}, bf16[16,16,512]{2,1,0:T(8,128)(2,1)S(1)}, u32[]{:S(2)}, u32[]{:S(2)}) collective-permute-start(bf16[16,16,512]{2,1,0:T(8,128)(2,1)S(1)} %get-tuple-element.18), channel_id=1, source_target_pairs={{0,128},{16,144},{32,160},{48,176},{64,192},{80,208},{96,224},{112... | collective-permute-start | bytes 786440 | tf_op jit(solution)/shard_map/ppermute | solution.py:244
  51.1 13.6 %collective-permute-start.7 = (bf16[8,32,1024]{2,1,0:T(8,128)(2,1)S(1)}, bf16[8,32,1024]{2,1,0:T(8,128)(2,1)S(1)}, u32[]{:S(2)}, u32[]{:S(2)}) collective-permute-start(bf16[8,32,1024]{2,1,0:T(8,128)(2,1)S(1)} %get-tuple-element.20), channel_id=1, source_target_pairs={{0,1},{1,0},{2,3},{3,2},{4,5},{5,4},{6,7},{7,6},{8,9},{9,8},{10,11... | collective-permute-start | bytes 1572872 | tf_op jit(solution)/shard_map/ppermute | solution.py:218
  52.0 35.0 %all-to-all-start.1 = ((bf16[16,48,512]{2,1,0:T(8,128)(2,1)}), bf16[16,48,512]{2,1,0:T(8,128)(2,1)S(1)}, u32[]{:S(2)}, u32[]{:S(2)}) async-start(bf16[16,48,512]{2,1,0:T(8,128)(2,1)} %fusion), calls=%async_computation.1 | async-start | bytes 1572864 | tf_op jit(solution)/shard_map/all_to_all | solution.py:277
  64.9 6.9 %collective-permute-start.10 = (bf16[2,32,1024]{2,1,0:T(8,128)(2,1)S(1)}, bf16[2,32,1024]{2,1,0:T(8,128)(2,1)S(1)}, u32[]{:S(2)}, u32[]{:S(2)}) collective-permute-start(bf16[2,32,1024]{2,1,0:T(8,128)(2,1)S(1)} %get-tuple-element.22), channel_id=1, source_target_pairs={{0,4},{1,5},{2,6},{3,7},{4,8},{5,9},{6,10},{7,11},{8,12},{9,13},{1... | collective-permute-start | bytes 393224 | tf_op jit(solution)/shard_map/ppermute | solution.py:218
  65.0 8.9 %collective-permute-start.8 = (bf16[2,32,1024]{2,1,0:T(8,128)(2,1)S(1)}, bf16[2,32,1024]{2,1,0:T(8,128)(2,1)S(1)}, u32[]{:S(2)}, u32[]{:S(2)}) collective-permute-start(bf16[2,32,1024]{2,1,0:T(8,128)(2,1)S(1)} %get-tuple-element.21), channel_id=1, source_target_pairs={{0,12},{1,13},{2,14},{3,15},{4,0},{5,1},{6,2},{7,3},{8,4},{9,5},{1... | collective-permute-start | bytes 393224 | tf_op jit(solution)/shard_map/ppermute | solution.py:218
  68.2 6.6 %collective-permute-start.9 = (bf16[2,32,1024]{2,1,0:T(8,128)(2,1)S(1)}, bf16[2,32,1024]{2,1,0:T(8,128)(2,1)S(1)}, u32[]{:S(2)}, u32[]{:S(2)}) collective-permute-start(bf16[2,32,1024]{2,1,0:T(8,128)(2,1)S(1)} %get-tuple-element.23), channel_id=1, source_target_pairs={{0,8},{1,9},{2,10},{3,11},{4,12},{5,13},{6,14},{7,15},{8,0},{9,1},... | collective-permute-start | bytes 393224 | tf_op jit(solution)/shard_map/ppermute | solution.py:218
  74.8 12.5 %collective-permute-start.11 = (bf16[32,1024]{1,0:T(8,128)(2,1)S(1)}, bf16[32,1024]{1,0:T(8,128)(2,1)S(1)}, u32[]{:S(2)}, u32[]{:S(2)}) collective-permute-start(bf16[32,1024]{1,0:T(8,128)(2,1)S(1)} %fusion.5), channel_id=1, source_target_pairs={{0,2},{1,3},{2,0},{3,1},{4,6},{5,7},{6,4},{7,5},{8,10},{9,11},{10,... | collective-permute-start | bytes 196616 | tf_op jit(solution)/shard_map/ppermute | solution.py:218

commit v5 on v4

--- a/solution.py
+++ b/solution.py
@@ -67,23 +67,28 @@
         lhs[s] = jnp.concatenate([u, q, jnp.ones((3, TB), bf16), pad], axis=0).T
 
 
-def tile_kernel(second, live_ref, list_ref, inv, lhs, zi1, cols, *refs):
+def tile_kernel(second, live_ref, list_ref, inv, lhs, cols, *refs):
     if second:
-        swapped, carry, tiles, rout, rout2, cout, w, sem, cacc, rhs, zj1, cb, racc = refs
+        zi1, swapped, carry, w, rout, rout2, cout, cacc, rhs, zj1, cb, racc = refs
     else:
-        tiles, racc, keep, send, w, sem, cacc, rhs, zj1, cb = refs
+        near, far, tiles, racc, keep, send, ahead, cacc, rhs, zj1, cb, w, sem, zi1 = refs
     y = lax.axis_index("row") >> 3
     mine, other = pl.multiple_of(y * FH, FH), pl.multiple_of((1 - y) * FH, FH)
     live = live_ref[0]
 
     def fetch(s):
-        return pltpu.make_async_copy(tiles.at[s, :, pl.ds(TJ if second else 0, TJ)], w.at[s], sem.at[s])
-
-    fetch(0).start()
-
-    @pl.when(1 < live)
-    def _():
-        fetch(1).start()
+        return pltpu.make_async_copy(tiles.at[s, :, pl.ds(0, TJ)], w.at[s], sem.at[s])
+
+    def fetch_ahead(s):
+        return pltpu.make_async_copy(tiles.at[s, :, pl.ds(TJ, TJ)], ahead.at[s], sem.at[S + s])
+
+    if not second:
+        fetch(0).start()
+
+        @pl.when(1 < live)
+        def _():
+            fetch(1).start()
+
 
     racc[...] = carry[...] if second else jnp.zeros(racc.shape, f32)
     cacc[...] = jnp.zeros(cacc.shape, f32)
@@ -97,6 +102,10 @@
         return row_place(list_ref, s), big_j & 15, scale
 
     def prepare(s, p):
+        if not second:
+            place = row_place(list_ref, s)
+            zi1[s, :F] = jnp.where(place < HALF, near[place & 7], far[place & 7])
+            zi1[s, F:] = ones_row(TB)
         jb = list_ref[2 * s + 1] & 15
         if second:
             zj1[p, pl.ds(mine, FH)] = cols[jb, F:]
@@ -126,11 +135,14 @@
         p = s & 1
         prev = jnp.maximum(s - 1, 0)
         now, old = slot(s), slot(prev)
-        fetch(s).wait()
-
-        @pl.when(s + 2 < live)
-        def _():
-            fetch(s + 2).start()
+        if not second:
+            fetch(s).wait()
+
+            @pl.when(s + 2 < live)
+            def _():
+                fetch(s + 2).start()
+
+            fetch_ahead(s).start()
 
         for n in range(NS):
             m, t, q, (ib, jb, scale) = (n - 1, s, p, now) if n else (NS - 1, prev, 1 - p, old)
@@ -165,6 +177,10 @@
         keep[...] = cacc[:, pl.ds(mine, FH)]
         send[...] = cacc[:, pl.ds(other, FH)].astype(bf16)
 
+        @pl.loop(0, live)
+        def _(s):
+            fetch_ahead(s).wait()
+
 
 SMEM = pl.BlockSpec(memory_space=pltpu.SMEM)
 VMEM = pl.BlockSpec(memory_space=pltpu.VMEM)
@@ -182,12 +198,10 @@
     )(live, tile_list, inv, near, far)
 
 
-def tile_pass(second, tiles, *args):
-    total = (N, F, TB)
+def tile_pass(second, *args):
+    total, tile = (N, F, TB), (S, TB, TJ)
     half = jax.ShapeDtypeStruct((HALF, F, TB), bf16)
     scratch = [
-        pltpu.VMEM((S, TB, TJ), bf16),
-        pltpu.SemaphoreType.DMA((S,)),
         pltpu.VMEM((N, F, TJ), f32),
         pltpu.VMEM((2, K, TJ), bf16),
         pltpu.VMEM((2, K, TJ), bf16),
@@ -197,7 +211,9 @@
         outs = [half, half, jax.ShapeDtypeStruct((N, F + FH, TJ), bf16)]
         scratch.append(pltpu.VMEM(total, f32))
     else:
-        outs = [jax.ShapeDtypeStruct(shape, t) for shape, t in ((total, f32), ((N, FH, TJ), f32), ((N, FH, TJ), bf16))]
+        scratch += [pltpu.VMEM(tile, bf16), pltpu.SemaphoreType.DMA((2 * S,)), pltpu.VMEM((S, K, TB), bf16)]
+        outs = [(total, f32), ((N, FH, TJ), f32), ((N, FH, TJ), bf16), (tile, bf16)]
+        outs = [jax.ShapeDtypeStruct(*out) for out in outs]
 
     def run(*refs):
         tile_kernel(second, *refs)
@@ -205,13 +221,13 @@
     return pl.pallas_call(
         run,
         out_shape=outs,
-        in_specs=[SMEM] * 2 + [VMEM] * (len(args) - 2) + [pl.BlockSpec(memory_space=pl.ANY)],
+        in_specs=[SMEM] * 2 + [VMEM] * (len(args) - 3) + [VMEM if second else pl.BlockSpec(memory_space=pl.ANY)],
         out_specs=[VMEM] * len(outs),
         scratch_shapes=scratch,
-        compiler_params=pltpu.CompilerParams(vmem_limit_bytes=44 * 1024 * 1024),
+        compiler_params=pltpu.CompilerParams(vmem_limit_bytes=40 * 1024 * 1024),
         cost_estimate=pl.CostEstimate(flops=10**10, bytes_accessed=10**7, transcendentals=0),
         name="second_half" if second else "first_half",
-    )(*args, tiles)
+    )(*args)
 
 
 def move(x, to):
@@ -249,10 +265,6 @@
         part = d // HALF * FH
         copies[d, :F] = block[:, :TJ]
         copies[d, F:] = block[part : part + FH, TJ:]
-
-
-def echo(block, copies, same):
-    same[...] = block[...]
 
 
 def gather_row(block):
@@ -263,14 +275,7 @@
         out_specs=VMEM,
         name="spread",
     )(block)
-    same = pl.pallas_call(
-        echo,
-        out_shape=jax.ShapeDtypeStruct((F, TB), bf16),
-        in_specs=[VMEM, pl.BlockSpec(memory_space=pl.ANY)],
-        out_specs=VMEM,
-        name="echo",
-    )(block, copies)
-    return lax.all_to_all(copies, "row", 0, 0, tiled=True), same
+    return lax.all_to_all(copies, "row", 0, 0, tiled=True)
 
 
 def scatter_row(parts):
@@ -283,14 +288,14 @@
 def body(features, inv_scales, inverse_tiles, tile_list, live_count):
     block = features[0, 0]
     live, places, inv = live_count.reshape(1), tile_list.reshape(2 * S), inv_scales.reshape(F, 1)
-    cols, block = gather_row(block)
+    cols = gather_row(block)
     near, far = gather_col(block)
     lhs, zi1 = prepare_pass(live, places, inv, near, far)
     swapped = swap_y(cols[:, F:])
     tiles = inverse_tiles[0, 0]
-    carry, keep, send = tile_pass(False, tiles, live, places, inv, lhs, zi1, cols)
+    carry, keep, send, ahead = tile_pass(False, live, places, inv, lhs, cols, near, far, tiles)
     got = swap_y(send)
-    rpart, rpart2, cpart = tile_pass(True, tiles, live, places, inv, lhs, zi1, cols, swapped, carry)
+    rpart, rpart2, cpart = tile_pass(True, live, places, inv, lhs, cols, zi1, swapped, carry, ahead)
     pair = (keep + got.astype(f32)).astype(bf16)
     cpart = lax.dynamic_update_slice(cpart, pair, (0, F, 0))
     total = scatter_row(cpart) + scatter_col(rpart, rpart2)

time: 88 us -> 82.1 us (0.933); the launches traced: 88.1 us -> 80.7 us
  starting transfers between devices: 39.2 us -> 32.5 us
  Pallas kernels: 13.5 us -> 16.4 us
  local copies, waits for them, and re-layouts: 3.11 us -> 1.2 us
    all_to_all x1, waiting for transfers between devices: 0.01 us -> 6.5 us  [gather_row(): return lax.all_to_all(copies, 'row', 0, 0, tiled=True)]
    ppermute x2, starting transfers between devices: 7.19 us -> 1.12 us  [swap_y(): return lax.ppermute(x, 'row', [(i, i ^ HALF) for i in range(N)])]
    ppermute x10, waiting for transfers between devices: 16.4 us -> 10.8 us  [move(): return lax.ppermute(x, 'col', [(i, to(i)) for i in range(N)])]
    ppermute x10, starting transfers between devices: 9.95 us -> 14.1 us  [move(): return lax.ppermute(x, 'col', [(i, to(i)) for i in range(N)])]
    all_to_all x1, starting transfers between devices: 12.7 us -> 8.64 us  [scatter_row(): got = lax.all_to_all(parts, 'row', 0, 0, tiled=True).astype(f32)]
    pallas_call x2, Pallas kernels: 9.23 us -> 13.1 us  [tile_pass(): pl.pallas_call(run, out_shape=outs, in_specs=[SMEM] * 2 + [VMEM] * (len(a...]
    all_to_all x1, waiting for transfers between devices: 12 us -> 9.96 us  [scatter_row(): got = lax.all_to_all(parts, 'row', 0, 0, tiled=True).astype(f32)]
    unnamed x13 -> x15, local copies, waits for them, and re-layouts: 2.88 us -> 0.96 us
  transfers between devices with their start and end apart: 14 -> 14, of which waited for: 9 -> 9; matrix products, arithmetic and copies ran while one was open for 4% -> 2% of each run, Pallas kernels for 13% -> 20%
where the time goes in v5:
time: 82.1 us; the launch traced here: 80.7 us
  starting transfers between devices  32.5 us (40%)
  waiting for transfers between devices  27.7 us (34%)
  Pallas kernels  16.4 us (20%)
  other arithmetic  2.12 us (3%)
  local copies, waits for them, and re-layouts  1.2 us (1%)
  between operations  0.86 us (1%)
    ppermute x10, starting transfers between devices, move(): return lax.ppermute(x, 'col', [(i, to(i)) for i in range(N)])  14.1 us
    pallas_call x2, Pallas kernels, tile_pass(): pl.pallas_call(run, out_shape=outs, in_specs=[SMEM] * 2 + [VMEM] * (len(a...  13.1 us
    ppermute x10, waiting for transfers between devices, move(): return lax.ppermute(x, 'col', [(i, to(i)) for i in range(N)])  10.8 us
    all_to_all x1, waiting for transfers between devices, scatter_row(): got = lax.all_to_all(parts, 'row', 0, 0, tiled=True).astype(f32)  9.96 us
    all_to_all x1, starting transfers between devices, scatter_row(): got = lax.all_to_all(parts, 'row', 0, 0, tiled=True).astype(f32)  8.64 us
    all_to_all x1, starting transfers between devices, gather_row(): return lax.all_to_all(copies, 'row', 0, 0, tiled=True)  8.58 us
    all_to_all x1, waiting for transfers between devices, gather_row(): return lax.all_to_all(copies, 'row', 0, 0, tiled=True)  6.5 us
    pallas_call x1, Pallas kernels, gather_row(): pl.pallas_call(spread, out_shape=jax.ShapeDtypeStruct((N, F + FH, TJ), bf...  1.81 us
  transfers between devices with their start and end apart: 14, of which 9 were waited for; matrix products, arithmetic and copies ran while one was open for 2% of the time, Pallas kernels for 20%

profile of v5, /device:TPU:16, one launch (start us, length us, event | category | flops | bytes accessed | tf_op | source)
XLA Modules:
  0.0 80.7 jit_solution(17677417384574799038)
XLA Ops:
  0.0 0.0 copy-start.2
  0.0 2.1 %collective-permute-start = (bf16[32,1024]{1,0:T(8,128)(2,1)}, bf16[32,1024]{1,0:T(8,128)(2,1)S(1)}, u32[]{:S(2)}, u32[]{:S(2)}) collective-permute-start(bf16[32,1024]{1,0:T(8,128)(2,1)} %bitcast.28), channel_id=1, source_target_pairs={{0,2},{1,3},{2,0},{3,1},{4,6},{5,7},{6,4},{7,5},{8,10},{9,11},{10,... | collective-permute-start | bytes 196616 | tf_op jit(solution)/shard_map/ppermute | solution.py:234
  2.1 1.8 %spread.1 = bf16[16,48,512]{2,1,0:T(8,128)(2,1)} custom-call(bf16[32,1024]{1,0:T(8,128)(2,1)} %bitcast.29), custom_call_target="tpu_custom_call" | custom-call | tf_op jit(solution)/shard_map/spread/pallas_call | solution.py:271
  3.9 0.0 copy-start.4
  3.9 0.0 copy-start.3
  3.9 8.6 %all-to-all-start = ((bf16[16,48,512]{2,1,0:T(8,128)(2,1)}), bf16[16,48,512]{2,1,0:T(8,128)(2,1)S(1)}, u32[]{:S(2)}, u32[]{:S(2)}) async-start(bf16[16,48,512]{2,1,0:T(8,128)(2,1)} %spread.1), calls=%async_computation | async-start | bytes 1572864 | tf_op jit(solution)/shard_map/all_to_all | solution.py:278
  12.5 0.0 copy-done.2
  12.5 0.0 collective-permute-done
  12.5 1.6 %collective-permute-start.1 = (bf16[2,32,1024]{2,1,0:T(8,128)(2,1)S(1)}, bf16[2,32,1024]{2,1,0:T(8,128)(2,1)S(1)}, u32[]{:S(2)}, u32[]{:S(2)}) collective-permute-start(bf16[2,32,1024]{2,1,0:T(8,128)(2,1)S(1)} %pad_maximum_fusion), channel_id=1, source_target_pairs={{0,4},{1,5},{2,6},{3,7},{4,8},{5,9},{6,10},{7,11},{8,12},{9,13},{1... | collective-permute-start | bytes 393224 | tf_op jit(solution)/shard_map/ppermute | solution.py:234
  14.1 2.7 %collective-permute-start.2 = (bf16[2,32,1024]{2,1,0:T(8,128)(2,1)S(1)}, bf16[2,32,1024]{2,1,0:T(8,128)(2,1)S(1)}, u32[]{:S(2)}, u32[]{:S(2)}) collective-permute-start(bf16[2,32,1024]{2,1,0:T(8,128)(2,1)S(1)} %pad_maximum_fusion), channel_id=1, source_target_pairs={{0,8},{1,9},{2,10},{3,11},{4,12},{5,13},{6,14},{7,15},{8,0},{9,1},... | collective-permute-start | bytes 393224 | tf_op jit(solution)/shard_map/ppermute | solution.py:234
  16.8 1.4 %collective-permute-start.3 = (bf16[2,32,1024]{2,1,0:T(8,128)(2,1)S(1)}, bf16[2,32,1024]{2,1,0:T(8,128)(2,1)S(1)}, u32[]{:S(2)}, u32[]{:S(2)}) collective-permute-start(bf16[2,32,1024]{2,1,0:T(8,128)(2,1)S(1)} %pad_maximum_fusion), channel_id=1, source_target_pairs={{0,12},{1,13},{2,14},{3,15},{4,0},{5,1},{6,2},{7,3},{8,4},{9,5},{1... | collective-permute-start | bytes 393224 | tf_op jit(solution)/shard_map/ppermute | solution.py:234
  18.3 1.6 %collective-permute-done.1 = bf16[2,32,1024]{2,1,0:T(8,128)(2,1)S(1)} collective-permute-done((bf16[2,32,1024]{2,1,0:T(8,128)(2,1)S(1)}, bf16[2,32,1024]{2,1,0:T(8,128)(2,1)S(1)}, u32[]{:S(2)}, u32[]{:S(2)}) %collective-permute-start.1) | collective-permute-done | bytes 131104 | tf_op jit(solution)/shard_map/ppermute | solution.py:234
  19.9 2.4 %collective-permute-done.2 = bf16[2,32,1024]{2,1,0:T(8,128)(2,1)S(1)} collective-permute-done((bf16[2,32,1024]{2,1,0:T(8,128)(2,1)S(1)}, bf16[2,32,1024]{2,1,0:T(8,128)(2,1)S(1)}, u32[]{:S(2)}, u32[]{:S(2)}) %collective-permute-start.2) | collective-permute-done | bytes 131104 | tf_op jit(solution)/shard_map/ppermute | solution.py:234
  22.3 0.0 collective-permute-done.3
  22.4 0.1 collective-permute-start.4
  22.5 0.0 copy-done.4
  22.5 0.1 copy.13.inv.refs_2_
  22.6 0.0 copy-done.3
  22.6 0.1 copy.10
  22.7 0.1 reshape.18.list_ref.refs_1_
  23.4 1.0 %collective-permute-done.4.far.refs_6_ = bf16[8,32,1024]{2,1,0:T(8,128)(2,1)S(1)} collective-permute-done((bf16[8,32,1024]{2,1,0:T(8,128)(2,1)S(1)}, bf16[8,32,1024]{2,1,0:T(8,128)(2,1)S(1)}, u32[]{:S(2)}, u32[]{:S(2)}) %collective-permute-start.4) | collective-permute-done | bytes 524320 | tf_op jit(solution)/shard_map/ppermute | solution.py:234
  24.4 1.5 %prepare_rows.1 = (bf16[6,1024,48]{2,1,0:T(8,128)(2,1)S(1)}, bf16[6,48,1024]{2,1,0:T(8,128)(2,1)S(1)}) custom-call(s32[1]{0:T(128)} %bitcast.25.live_ref, s32[12]{0:T(128)S(1)} %reshape.18.list_ref.refs_1_, f32[32,1]{1,0:T(8,128)S(1)} %copy.13.inv.refs_2_, bf16[8,32,1024]{2,1,0:T(8,128)(2,1)S(1)} %constant_dynamic-update-slice_fusion.near.refs_5_, ...), custom_call_target="tpu_custom_call" | custom-call | flops 2000000000 | bytes 1000000 | tf_op jit(solution)/shard_map/prepare_rows/pallas_call | solution.py:190
  25.8 0.0 copy-start
  25.8 0.8 %copy-done = bf16[6,48,1024]{2,1,0:T(8,128)(2,1)} copy-done((bf16[6,48,1024]{2,1,0:T(8,128)(2,1)}, bf16[6,48,1024]{2,1,0:T(8,128)(2,1)S(1)}, u32[]{:S(2)}) %copy-start) | copy-done | bytes 589848
  26.7 6.5 %all-to-all-done.refs_4_ = bf16[16,48,512]{2,1,0:T(8,128)(2,1)S(1)} async-done(((bf16[16,48,512]{2,1,0:T(8,128)(2,1)}), bf16[16,48,512]{2,1,0:T(8,128)(2,1)S(1)}, u32[]{:S(2)}, u32[]{:S(2)}) %all-to-all-start) | async-done | bytes 786464 | tf_op jit(solution)/shard_map/all_to_all | solution.py:278
  33.2 1.0 %collective-permute-start.5 = (bf16[16,16,512]{2,1,0:T(8,128)(2,1)S(1)}, bf16[16,16,512]{2,1,0:T(8,128)(2,1)S(1)}, u32[]{:S(2)}, u32[]{:S(2)}) collective-permute-start(bf16[16,16,512]{2,1,0:T(8,128)(2,1)S(1)} %slice.37), channel_id=1, source_target_pairs={{0,128},{16,144},{32,160},{48,176},{64,192},{80,208},{96,224},{112... | collective-permute-start | bytes 786440 | tf_op jit(solution)/shard_map/ppermute | solution.py:260
  34.2 0.0 copy-start.1
  34.2 7.1 %first_half.1 = (f32[16,32,1024]{2,1,0:T(8,128)S(1)}, f32[16,16,512]{2,1,0:T(8,128)S(1)}, bf16[16,16,512]{2,1,0:T(8,128)(2,1)S(1)}, bf16[6,1024,512]{2,1,0:T(8,128)(2,1)S(1)}) custom-call(s32[1]{0:T(128)} %bitcast.26.refs_0_, s32[12]{0:T(128)S(1)} %reshape.18.list_ref.refs_1_, f32[32,1]{1,0:T(8,128)S(1)} %copy.13.inv.refs_2_, ...), custom_call_target="tpu_custom_call" | custom-call | flops 10000000000 | bytes 10000000 | tf_op jit(solution)/shard_map/first_half/pallas_call | solution.py:221
  41.4 0.1 collective-permute-start.6
  41.5 0.0 collective-permute-done.5.refs_6_
  41.5 0.0 copy-done.1
  41.5 6.0 %second_half.1 = (bf16[8,32,1024]{2,1,0:T(8,128)(2,1)S(1)}, bf16[8,32,1024]{2,1,0:T(8,128)(2,1)S(1)}, bf16[16,48,512]{2,1,0:T(8,128)(2,1)}) custom-call(s32[1]{0:T(128)} %bitcast.27.refs_0_, s32[12]{0:T(128)S(1)} %reshape.18.list_ref.refs_1_, f32[32,1]{1,0:T(8,128)S(1)} %copy.13.inv.refs_2_, bf16[6,1024,48]{2,1,0:T(8,128)(2,1)S(1)} %get-tuple-element.14.refs_3_, ...), custom_call_target="tpu_custom_call" | custom-call | flops 10000000000 | bytes 10000000 | tf_op jit(solution)/shard_map/second_half/pallas_call | solution.py:221
  47.5 0.0 collective-permute-start.7
  47.5 0.3 collective-permute-done.6
  47.8 0.8 fusion
  48.6 8.6 %all-to-all-start.1 = ((bf16[16,48,512]{2,1,0:T(8,128)(2,1)}), bf16[16,48,512]{2,1,0:T(8,128)(2,1)S(1)}, u32[]{:S(2)}, u32[]{:S(2)}) async-start(bf16[16,48,512]{2,1,0:T(8,128)(2,1)} %fusion), calls=%async_computation.1 | async-start | bytes 1572864 | tf_op jit(solution)/shard_map/all_to_all | solution.py:282
  57.3 0.0 collective-permute-done.7
  57.3 0.2 add_convert_fusion
  57.5 1.1 %collective-permute-start.10 = (bf16[2,32,1024]{2,1,0:T(8,128)(2,1)S(1)}, bf16[2,32,1024]{2,1,0:T(8,128)(2,1)S(1)}, u32[]{:S(2)}, u32[]{:S(2)}) collective-permute-start(bf16[2,32,1024]{2,1,0:T(8,128)(2,1)S(1)} %get-tuple-element.24), channel_id=1, source_target_pairs={{0,4},{1,5},{2,6},{3,7},{4,8},{5,9},{6,10},{7,11},{8,12},{9,13},{1... | collective-permute-start | bytes 393224 | tf_op jit(solution)/shard_map/ppermute | solution.py:234
  58.6 2.2 %collective-permute-start.8 = (bf16[2,32,1024]{2,1,0:T(8,128)(2,1)S(1)}, bf16[2,32,1024]{2,1,0:T(8,128)(2,1)S(1)}, u32[]{:S(2)}, u32[]{:S(2)}) collective-permute-start(bf16[2,32,1024]{2,1,0:T(8,128)(2,1)S(1)} %get-tuple-element.23), channel_id=1, source_target_pairs={{0,12},{1,13},{2,14},{3,15},{4,0},{5,1},{6,2},{7,3},{8,4},{9,5},{1... | collective-permute-start | bytes 393224 | tf_op jit(solution)/shard_map/ppermute | solution.py:234
  60.8 1.1 %collective-permute-start.9 = (bf16[2,32,1024]{2,1,0:T(8,128)(2,1)S(1)}, bf16[2,32,1024]{2,1,0:T(8,128)(2,1)S(1)}, u32[]{:S(2)}, u32[]{:S(2)}) collective-permute-start(bf16[2,32,1024]{2,1,0:T(8,128)(2,1)S(1)} %get-tuple-element.25), channel_id=1, source_target_pairs={{0,8},{1,9},{2,10},{3,11},{4,12},{5,13},{6,14},{7,15},{8,0},{9,1},... | collective-permute-start | bytes 393224 | tf_op jit(solution)/shard_map/ppermute | solution.py:234
  62.0 2.5 %collective-permute-done.10 = bf16[2,32,1024]{2,1,0:T(8,128)(2,1)S(1)} collective-permute-done((bf16[2,32,1024]{2,1,0:T(8,128)(2,1)S(1)}, bf16[2,32,1024]{2,1,0:T(8,128)(2,1)S(1)}, u32[]{:S(2)}, u32[]{:S(2)}) %collective-permute-start.10) | collective-permute-done | bytes 131104 | tf_op jit(solution)/shard_map/ppermute | solution.py:234
  64.4 2.1 %collective-permute-done.8 = bf16[2,32,1024]{2,1,0:T(8,128)(2,1)S(1)} collective-permute-done((bf16[2,32,1024]{2,1,0:T(8,128)(2,1)S(1)}, bf16[2,32,1024]{2,1,0:T(8,128)(2,1)S(1)}, u32[]{:S(2)}, u32[]{:S(2)}) %collective-permute-start.8) | collective-permute-done | bytes 131104 | tf_op jit(solution)/shard_map/ppermute | solution.py:234
  66.5 1.3 %collective-permute-done.9 = bf16[2,32,1024]{2,1,0:T(8,128)(2,1)S(1)} collective-permute-done((bf16[2,32,1024]{2,1,0:T(8,128)(2,1)S(1)}, bf16[2,32,1024]{2,1,0:T(8,128)(2,1)S(1)}, u32[]{:S(2)}, u32[]{:S(2)}) %collective-permute-start.9) | collective-permute-done | bytes 131104 | tf_op jit(solution)/shard_map/ppermute | solution.py:234
  67.8 0.1 convert_add_fusion
  67.9 1.8 %collective-permute-start.11 = (bf16[32,1024]{1,0:T(8,128)(2,1)S(1)}, bf16[32,1024]{1,0:T(8,128)(2,1)S(1)}, u32[]{:S(2)}, u32[]{:S(2)}) collective-permute-start(bf16[32,1024]{1,0:T(8,128)(2,1)S(1)} %fusion.5), channel_id=1, source_target_pairs={{0,2},{1,3},{2,0},{3,1},{4,6},{5,7},{6,4},{7,5},{8,10},{9,11},{10,... | collective-permute-start | bytes 196616 | tf_op jit(solution)/shard_map/ppermute | solution.py:234
  69.7 10.0 %all-to-all-done.1 = bf16[16,48,512]{2,1,0:T(8,128)(2,1)S(1)} async-done(((bf16[16,48,512]{2,1,0:T(8,128)(2,1)}), bf16[16,48,512]{2,1,0:T(8,128)(2,1)S(1)}, u32[]{:S(2)}, u32[]{:S(2)}) %all-to-all-start.1) | async-done | bytes 786464 | tf_op jit(solution)/shard_map/all_to_all | solution.py:282
  79.6 0.2 convert_element_type.39
  79.8 0.1 slice_reduce_fusion
  80.0 0.0 collective-permute-done.11
  80.0 0.7 fusion.4
  (11 shorter events, 0.2 us)
Async XLA Ops:
  0.0 12.5 %copy-start.2 = (bf16[1,1,32,1024]{3,2,1,0:T(8,128)(2,1)S(1)}, bf16[1,1,32,1024]{3,2,1,0:T(8,128)(2,1)}, u32[]{:S(2)}) copy-start(bf16[1,1,32,1024]{3,2,1,0:T(8,128)(2,1)} %param.5) | copy-start | bytes 196612
  0.0 12.5 %collective-permute-start = (bf16[32,1024]{1,0:T(8,128)(2,1)}, bf16[32,1024]{1,0:T(8,128)(2,1)S(1)}, u32[]{:S(2)}, u32[]{:S(2)}) collective-permute-start(bf16[32,1024]{1,0:T(8,128)(2,1)} %bitcast.28), channel_id=1, source_target_pairs={{0,2},{1,3},{2,0},{3,1},{4,6},{5,7},{6,4},{7,5},{8,10},{9,11},{10,... | collective-permute-start | bytes 196616 | tf_op jit(solution)/shard_map/ppermute | solution.py:234
  3.9 18.6 %copy-start.4 = (f32[32]{0:T(128)S(1)}, f32[32]{0:T(128)}, u32[]{:S(2)}) copy-start(f32[32]{0:T(128)} %param.6) | copy-start | bytes 388
  3.9 18.7 %copy-start.3 = (s32[1,1,6,2]{2,3,1,0:T(2,128)S(1)}, s32[1,1,6,2]{2,3,1,0:T(2,128)}, u32[]{:S(2)}) copy-start(s32[1,1,6,2]{2,3,1,0:T(2,128)} %param.8) | copy-start | bytes 148
  3.9 29.3 %all-to-all-start = ((bf16[16,48,512]{2,1,0:T(8,128)(2,1)}), bf16[16,48,512]{2,1,0:T(8,128)(2,1)S(1)}, u32[]{:S(2)}, u32[]{:S(2)}) async-start(bf16[16,48,512]{2,1,0:T(8,128)(2,1)} %spread.1), calls=%async_computation | async-start | bytes 1572864 | tf_op jit(solution)/shard_map/all_to_all | solution.py:278
  12.5 7.3 %collective-permute-start.1 = (bf16[2,32,1024]{2,1,0:T(8,128)(2,1)S(1)}, bf16[2,32,1024]{2,1,0:T(8,128)(2,1)S(1)}, u32[]{:S(2)}, u32[]{:S(2)}) collective-permute-start(bf16[2,32,1024]{2,1,0:T(8,128)(2,1)S(1)} %pad_maximum_fusion), channel_id=1, source_target_pairs={{0,4},{1,5},{2,6},{3,7},{4,8},{5,9},{6,10},{7,11},{8,12},{9,13},{1... | collective-permute-start | bytes 393224 | tf_op jit(solution)/shard_map/ppermute | solution.py:234
  14.1 8.2 %collective-permute-start.2 = (bf16[2,32,1024]{2,1,0:T(8,128)(2,1)S(1)}, bf16[2,32,1024]{2,1,0:T(8,128)(2,1)S(1)}, u32[]{:S(2)}, u32[]{:S(2)}) collective-permute-start(bf16[2,32,1024]{2,1,0:T(8,128)(2,1)S(1)} %pad_maximum_fusion), channel_id=1, source_target_pairs={{0,8},{1,9},{2,10},{3,11},{4,12},{5,13},{6,14},{7,15},{8,0},{9,1},... | collective-permute-start | bytes 393224 | tf_op jit(solution)/shard_map/ppermute | solution.py:234
  16.8 5.5 %collective-permute-start.3 = (bf16[2,32,1024]{2,1,0:T(8,128)(2,1)S(1)}, bf16[2,32,1024]{2,1,0:T(8,128)(2,1)S(1)}, u32[]{:S(2)}, u32[]{:S(2)}) collective-permute-start(bf16[2,32,1024]{2,1,0:T(8,128)(2,1)S(1)} %pad_maximum_fusion), channel_id=1, source_target_pairs={{0,12},{1,13},{2,14},{3,15},{4,0},{5,1},{6,2},{7,3},{8,4},{9,5},{1... | collective-permute-start | bytes 393224 | tf_op jit(solution)/shard_map/ppermute | solution.py:234
  22.4 2.0 %collective-permute-start.4 = (bf16[8,32,1024]{2,1,0:T(8,128)(2,1)S(1)}, bf16[8,32,1024]{2,1,0:T(8,128)(2,1)S(1)}, u32[]{:S(2)}, u32[]{:S(2)}) collective-permute-start(bf16[8,32,1024]{2,1,0:T(8,128)(2,1)S(1)} %constant_dynamic-update-slice_fusion.near.refs_5_), channel_id=1, source_target_pairs={{0,1},{1,0},{2,3},{3,2},{4,5},{5,4},{6,7},{7,6},{8,9},{9,8},{10,11... | collective-permute-start | bytes 1572872 | tf_op jit(solution)/shard_map/ppermute | solution.py:234
  25.8 0.8 %copy-start = (bf16[6,48,1024]{2,1,0:T(8,128)(2,1)}, bf16[6,48,1024]{2,1,0:T(8,128)(2,1)S(1)}, u32[]{:S(2)}) copy-start(bf16[6,48,1024]{2,1,0:T(8,128)(2,1)S(1)} %get-tuple-element.15.refs_5_) | copy-start | bytes 1769476
  33.2 8.3 %collective-permute-start.5 = (bf16[16,16,512]{2,1,0:T(8,128)(2,1)S(1)}, bf16[16,16,512]{2,1,0:T(8,128)(2,1)S(1)}, u32[]{:S(2)}, u32[]{:S(2)}) collective-permute-start(bf16[16,16,512]{2,1,0:T(8,128)(2,1)S(1)} %slice.37), channel_id=1, source_target_pairs={{0,128},{16,144},{32,160},{48,176},{64,192},{80,208},{96,224},{112... | collective-permute-start | bytes 786440 | tf_op jit(solution)/shard_map/ppermute | solution.py:260
  34.2 7.3 %copy-start.1 = (bf16[6,48,1024]{2,1,0:T(8,128)(2,1)S(1)}, bf16[6,48,1024]{2,1,0:T(8,128)(2,1)}, u32[]{:S(2)}) copy-start(bf16[6,48,1024]{2,1,0:T(8,128)(2,1)} %copy-done) | copy-start | bytes 1769476
  41.4 6.5 %collective-permute-start.6 = (bf16[16,16,512]{2,1,0:T(8,128)(2,1)S(1)}, bf16[16,16,512]{2,1,0:T(8,128)(2,1)S(1)}, u32[]{:S(2)}, u32[]{:S(2)}) collective-permute-start(bf16[16,16,512]{2,1,0:T(8,128)(2,1)S(1)} %get-tuple-element.20), channel_id=1, source_target_pairs={{0,128},{16,144},{32,160},{48,176},{64,192},{80,208},{96,224},{112... | collective-permute-start | bytes 786440 | tf_op jit(solution)/shard_map/ppermute | solution.py:260
  47.5 9.8 %collective-permute-start.7 = (bf16[8,32,1024]{2,1,0:T(8,128)(2,1)S(1)}, bf16[8,32,1024]{2,1,0:T(8,128)(2,1)S(1)}, u32[]{:S(2)}, u32[]{:S(2)}) collective-permute-start(bf16[8,32,1024]{2,1,0:T(8,128)(2,1)S(1)} %get-tuple-element.22), channel_id=1, source_target_pairs={{0,1},{1,0},{2,3},{3,2},{4,5},{5,4},{6,7},{7,6},{8,9},{9,8},{10,11... | collective-permute-start | bytes 1572872 | tf_op jit(solution)/shard_map/ppermute | solution.py:234
  48.6 31.0 %all-to-all-start.1 = ((bf16[16,48,512]{2,1,0:T(8,128)(2,1)}), bf16[16,48,512]{2,1,0:T(8,128)(2,1)S(1)}, u32[]{:S(2)}, u32[]{:S(2)}) async-start(bf16[16,48,512]{2,1,0:T(8,128)(2,1)} %fusion), calls=%async_computation.1 | async-start | bytes 1572864 | tf_op jit(solution)/shard_map/all_to_all | solution.py:282
  57.5 6.9 %collective-permute-start.10 = (bf16[2,32,1024]{2,1,0:T(8,128)(2,1)S(1)}, bf16[2,32,1024]{2,1,0:T(8,128)(2,1)S(1)}, u32[]{:S(2)}, u32[]{:S(2)}) collective-permute-start(bf16[2,32,1024]{2,1,0:T(8,128)(2,1)S(1)} %get-tuple-element.24), channel_id=1, source_target_pairs={{0,4},{1,5},{2,6},{3,7},{4,8},{5,9},{6,10},{7,11},{8,12},{9,13},{1... | collective-permute-start | bytes 393224 | tf_op jit(solution)/shard_map/ppermute | solution.py:234
  58.6 7.9 %collective-permute-start.8 = (bf16[2,32,1024]{2,1,0:T(8,128)(2,1)S(1)}, bf16[2,32,1024]{2,1,0:T(8,128)(2,1)S(1)}, u32[]{:S(2)}, u32[]{:S(2)}) collective-permute-start(bf16[2,32,1024]{2,1,0:T(8,128)(2,1)S(1)} %get-tuple-element.23), channel_id=1, source_target_pairs={{0,12},{1,13},{2,14},{3,15},{4,0},{5,1},{6,2},{7,3},{8,4},{9,5},{1... | collective-permute-start | bytes 393224 | tf_op jit(solution)/shard_map/ppermute | solution.py:234
  60.8 7.0 %collective-permute-start.9 = (bf16[2,32,1024]{2,1,0:T(8,128)(2,1)S(1)}, bf16[2,32,1024]{2,1,0:T(8,128)(2,1)S(1)}, u32[]{:S(2)}, u32[]{:S(2)}) collective-permute-start(bf16[2,32,1024]{2,1,0:T(8,128)(2,1)S(1)} %get-tuple-element.25), channel_id=1, source_target_pairs={{0,8},{1,9},{2,10},{3,11},{4,12},{5,13},{6,14},{7,15},{8,0},{9,1},... | collective-permute-start | bytes 393224 | tf_op jit(solution)/shard_map/ppermute | solution.py:234
  67.9 12.1 %collective-permute-start.11 = (bf16[32,1024]{1,0:T(8,128)(2,1)S(1)}, bf16[32,1024]{1,0:T(8,128)(2,1)S(1)}, u32[]{:S(2)}, u32[]{:S(2)}) collective-permute-start(bf16[32,1024]{1,0:T(8,128)(2,1)S(1)} %fusion.5), channel_id=1, source_target_pairs={{0,2},{1,3},{2,0},{3,1},{4,6},{5,7},{6,4},{7,5},{8,10},{9,11},{10,... | collective-permute-start | bytes 196616 | tf_op jit(solution)/shard_map/ppermute | solution.py:234

commit v6 on v5

--- a/solution.py
+++ b/solution.py
@@ -71,24 +71,17 @@
     if second:
         zi1, swapped, carry, w, rout, rout2, cout, cacc, rhs, zj1, cb, racc = refs
     else:
-        near, far, tiles, racc, keep, send, ahead, cacc, rhs, zj1, cb, w, sem, zi1 = refs
+        near, far, tiles, racc, keep, send, w, cacc, rhs, zj1, cb, sem, zi1 = refs
     y = lax.axis_index("row") >> 3
     mine, other = pl.multiple_of(y * FH, FH), pl.multiple_of((1 - y) * FH, FH)
     live = live_ref[0]
+    start = TJ if second else 0
 
     def fetch(s):
-        return pltpu.make_async_copy(tiles.at[s, :, pl.ds(0, TJ)], w.at[s], sem.at[s])
-
-    def fetch_ahead(s):
-        return pltpu.make_async_copy(tiles.at[s, :, pl.ds(TJ, TJ)], ahead.at[s], sem.at[S + s])
+        return pltpu.make_async_copy(tiles.at[s], w.at[s], sem.at[s])
 
     if not second:
         fetch(0).start()
-
-        @pl.when(1 < live)
-        def _():
-            fetch(1).start()
-
 
     racc[...] = carry[...] if second else jnp.zeros(racc.shape, f32)
     cacc[...] = jnp.zeros(cacc.shape, f32)
@@ -130,6 +123,12 @@
 
     prepare(0, 0)
 
+    if not second:
+
+        @pl.when(1 < live)
+        def _():
+            fetch(1).start()
+
     @pl.loop(0, live)
     def _(s):
         p = s & 1
@@ -141,8 +140,6 @@
             @pl.when(s + 2 < live)
             def _():
                 fetch(s + 2).start()
-
-            fetch_ahead(s).start()
 
         for n in range(NS):
             m, t, q, (ib, jb, scale) = (n - 1, s, p, now) if n else (NS - 1, prev, 1 - p, old)
@@ -157,7 +154,7 @@
                     d = sq * lax.rsqrt(sq)
                     e = jnp.exp2(d * (-ROOT5 * LOG2E))
                     g = ((d + 1.0 / ROOT5) * e).astype(bf16)
-                    cb[n, h * SUB : (h + 1) * SUB, js] = g * w[s, at, js]
+                    cb[n, h * SUB : (h + 1) * SUB, js] = g * w[s, at, pl.ds(start + jc * CJ, CJ)]
             finish(m, t, ib, scale, rt)
             if n == NS - 1:
                 prepare(jnp.minimum(s + 1, live - 1), 1 - p)
@@ -177,10 +174,6 @@
         keep[...] = cacc[:, pl.ds(mine, FH)]
         send[...] = cacc[:, pl.ds(other, FH)].astype(bf16)
 
-        @pl.loop(0, live)
-        def _(s):
-            fetch_ahead(s).wait()
-
 
 SMEM = pl.BlockSpec(memory_space=pltpu.SMEM)
 VMEM = pl.BlockSpec(memory_space=pltpu.VMEM)
@@ -199,7 +192,7 @@
 
 
 def tile_pass(second, *args):
-    total, tile = (N, F, TB), (S, TB, TJ)
+    total, tile = (N, F, TB), (S, TB, TB)
     half = jax.ShapeDtypeStruct((HALF, F, TB), bf16)
     scratch = [
         pltpu.VMEM((N, F, TJ), f32),
@@ -211,7 +204,7 @@
         outs = [half, half, jax.ShapeDtypeStruct((N, F + FH, TJ), bf16)]
         scratch.append(pltpu.VMEM(total, f32))
     else:
-        scratch += [pltpu.VMEM(tile, bf16), pltpu.SemaphoreType.DMA((2 * S,)), pltpu.VMEM((S, K, TB), bf16)]
+        scratch += [pltpu.SemaphoreType.DMA((S,)), pltpu.VMEM((S, K, TB), bf16)]
         outs = [(total, f32), ((N, FH, TJ), f32), ((N, FH, TJ), bf16), (tile, bf16)]
         outs = [jax.ShapeDtypeStruct(*out) for out in outs]
 
@@ -224,7 +217,7 @@
         in_specs=[SMEM] * 2 + [VMEM] * (len(args) - 3) + [VMEM if second else pl.BlockSpec(memory_space=pl.ANY)],
         out_specs=[VMEM] * len(outs),
         scratch_shapes=scratch,
-        compiler_params=pltpu.CompilerParams(vmem_limit_bytes=40 * 1024 * 1024),
+        compiler_params=pltpu.CompilerParams(vmem_limit_bytes=32 * 1024 * 1024),
         cost_estimate=pl.CostEstimate(flops=10**10, bytes_accessed=10**7, transcendentals=0),
         name="second_half" if second else "first_half",
     )(*args)
@@ -260,22 +253,10 @@
     return lax.ppermute(x, "row", [(i, i ^ HALF) for i in range(N)])
 
 
-def spread(block, copies):
-    for d in range(N):
-        part = d // HALF * FH
-        copies[d, :F] = block[:, :TJ]
-        copies[d, F:] = block[part : part + FH, TJ:]
-
-
 def gather_row(block):
-    copies = pl.pallas_call(
-        spread,
-        out_shape=jax.ShapeDtypeStruct((N, F + FH, TJ), bf16),
-        in_specs=[VMEM],
-        out_specs=VMEM,
-        name="spread",
-    )(block)
-    return lax.all_to_all(copies, "row", 0, 0, tiled=True)
+    whole = jnp.broadcast_to(block[None, :, :TJ], (N, F, TJ))
+    part = jnp.broadcast_to(block[:, TJ:].reshape(2, 1, FH, TJ), (2, HALF, FH, TJ)).reshape(N, FH, TJ)
+    return lax.all_to_all(jnp.concatenate([whole, part], axis=1), "row", 0, 0, tiled=True)
 
 
 def scatter_row(parts):
@@ -293,9 +274,9 @@
     lhs, zi1 = prepare_pass(live, places, inv, near, far)
     swapped = swap_y(cols[:, F:])
     tiles = inverse_tiles[0, 0]
-    carry, keep, send, ahead = tile_pass(False, live, places, inv, lhs, cols, near, far, tiles)
+    carry, keep, send, held = tile_pass(False, live, places, inv, lhs, cols, near, far, tiles)
     got = swap_y(send)
-    rpart, rpart2, cpart = tile_pass(True, live, places, inv, lhs, cols, zi1, swapped, carry, ahead)
+    rpart, rpart2, cpart = tile_pass(True, live, places, inv, lhs, cols, zi1, swapped, carry, held)
     pair = (keep + got.astype(f32)).astype(bf16)
     cpart = lax.dynamic_update_slice(cpart, pair, (0, F, 0))
     total = scatter_row(cpart) + scatter_col(rpart, rpart2)

time: 82.1 us -> 82.5 us (level)
  Pallas kernels: 16.4 us -> 14.6 us
  starting transfers between devices: 32.5 us -> 33.6 us
  other arithmetic: 2.12 us -> 3.07 us
  waiting for transfers between devices: 27.7 us -> 26.8 us
  local copies, waits for them, and re-layouts: 1.2 us -> 2.05 us
    pallas_call x1 -> x0, Pallas kernels: 1.81 us -> none  [gather_row(): pl.pallas_call(spread, out_shape=jax.ShapeDtypeStruct((N, F + FH, TJ), bf...]
    concatenate x0 -> x1, other arithmetic: none -> 0.95 us  [gather_row(): jnp.concatenate([whole, part], axis=1)]
  transfers between devices with their start and end apart: 14 -> 14, of which waited for: 9 -> 9; matrix products, arithmetic and copies ran while one was open for 2% -> 4% of each run, Pallas kernels for 20% -> 18%
where the time goes in v6:
time: 82.5 us; the launch traced here: 80.9 us
  starting transfers between devices  33.6 us (41%)
  waiting for transfers between devices  26.8 us (32%)
  Pallas kernels  14.6 us (18%)
  other arithmetic  3.07 us (4%)
  local copies, waits for them, and re-layouts  2.05 us (2%)
  between operations  0.89 us (1%)
    ppermute x10, starting transfers between devices, move(): return lax.ppermute(x, 'col', [(i, to(i)) for i in range(N)])  14.8 us
    pallas_call x2, Pallas kernels, tile_pass(): pl.pallas_call(run, out_shape=outs, in_specs=[SMEM] * 2 + [VMEM] * (len(a...  13.1 us
    ppermute x10, waiting for transfers between devices, move(): return lax.ppermute(x, 'col', [(i, to(i)) for i in range(N)])  10.2 us
    all_to_all x1, waiting for transfers between devices, scatter_row(): got = lax.all_to_all(parts, 'row', 0, 0, tiled=True).astype(f32)  9.95 us
    all_to_all x1, starting transfers between devices, scatter_row(): got = lax.all_to_all(parts, 'row', 0, 0, tiled=True).astype(f32)  9.09 us
    all_to_all x1, starting transfers between devices, gather_row(): lax.all_to_all(jnp.concatenate([whole, part], axis=1), 'row', 0, 0, tiled...  8.58 us
    all_to_all x1, waiting for transfers between devices, gather_row(): lax.all_to_all(jnp.concatenate([whole, part], axis=1), 'row', 0, 0, tiled...  6.51 us
  transfers between devices with their start and end apart: 14, of which 9 were waited for; matrix products, arithmetic and copies ran while one was open for 4% of the time, Pallas kernels for 18%

profile of v6, /device:TPU:16, one launch (start us, length us, event | category | flops | bytes accessed | tf_op | source)
XLA Modules:
  0.0 80.9 jit_solution(15526468764250318978)
XLA Ops:
  0.0 2.1 %collective-permute-start = (bf16[32,1024]{1,0:T(8,128)(2,1)}, bf16[32,1024]{1,0:T(8,128)(2,1)S(1)}, u32[]{:S(2)}, u32[]{:S(2)}) collective-permute-start(bf16[32,1024]{1,0:T(8,128)(2,1)} %bitcast.31), channel_id=1, source_target_pairs={{0,2},{1,3},{2,0},{3,1},{4,6},{5,7},{6,4},{7,5},{8,10},{9,11},{10,... | collective-permute-start | bytes 196616 | tf_op jit(solution)/shard_map/ppermute | solution.py:227
  2.1 0.8 fusion.7
  2.9 0.0 copy-start.2
  3.0 0.9 %pad_maximum_fusion = bf16[16,48,512]{2,1,0:T(8,128)(2,1)} fusion(bf16[16,16,512]{2,1,0:T(8,128)(2,1)S(1)} %bitcast.30, bf16[16,32,512]{2,1,0:T(8,128)(2,1)S(1)} %broadcast_in_dim.8), kind=kLoop, calls=%fused_computation.2 | loop fusion | flops 1572864 | bytes 1572864 | tf_op jit(solution)/shard_map/concatenate | solution.py:259
  3.9 0.0 copy-start.4
  3.9 0.0 copy-start.3
  3.9 8.6 %all-to-all-start = ((bf16[16,48,512]{2,1,0:T(8,128)(2,1)}), bf16[16,48,512]{2,1,0:T(8,128)(2,1)S(1)}, u32[]{:S(2)}, u32[]{:S(2)}) async-start(bf16[16,48,512]{2,1,0:T(8,128)(2,1)} %pad_maximum_fusion), calls=%async_computation | async-start | bytes 1572864 | tf_op jit(solution)/shard_map/all_to_all | solution.py:259
  12.5 0.0 copy-done.2
  12.5 0.0 collective-permute-done
  12.6 1.6 %collective-permute-start.1 = (bf16[2,32,1024]{2,1,0:T(8,128)(2,1)S(1)}, bf16[2,32,1024]{2,1,0:T(8,128)(2,1)S(1)}, u32[]{:S(2)}, u32[]{:S(2)}) collective-permute-start(bf16[2,32,1024]{2,1,0:T(8,128)(2,1)S(1)} %pad_maximum_fusion.1), channel_id=1, source_target_pairs={{0,4},{1,5},{2,6},{3,7},{4,8},{5,9},{6,10},{7,11},{8,12},{9,13},{1... | collective-permute-start | bytes 393224 | tf_op jit(solution)/shard_map/ppermute | solution.py:227
  14.1 2.7 %collective-permute-start.2 = (bf16[2,32,1024]{2,1,0:T(8,128)(2,1)S(1)}, bf16[2,32,1024]{2,1,0:T(8,128)(2,1)S(1)}, u32[]{:S(2)}, u32[]{:S(2)}) collective-permute-start(bf16[2,32,1024]{2,1,0:T(8,128)(2,1)S(1)} %pad_maximum_fusion.1), channel_id=1, source_target_pairs={{0,8},{1,9},{2,10},{3,11},{4,12},{5,13},{6,14},{7,15},{8,0},{9,1},... | collective-permute-start | bytes 393224 | tf_op jit(solution)/shard_map/ppermute | solution.py:227
  16.9 1.4 %collective-permute-start.3 = (bf16[2,32,1024]{2,1,0:T(8,128)(2,1)S(1)}, bf16[2,32,1024]{2,1,0:T(8,128)(2,1)S(1)}, u32[]{:S(2)}, u32[]{:S(2)}) collective-permute-start(bf16[2,32,1024]{2,1,0:T(8,128)(2,1)S(1)} %pad_maximum_fusion.1), channel_id=1, source_target_pairs={{0,12},{1,13},{2,14},{3,15},{4,0},{5,1},{6,2},{7,3},{8,4},{9,5},{1... | collective-permute-start | bytes 393224 | tf_op jit(solution)/shard_map/ppermute | solution.py:227
  18.3 1.6 %collective-permute-done.1 = bf16[2,32,1024]{2,1,0:T(8,128)(2,1)S(1)} collective-permute-done((bf16[2,32,1024]{2,1,0:T(8,128)(2,1)S(1)}, bf16[2,32,1024]{2,1,0:T(8,128)(2,1)S(1)}, u32[]{:S(2)}, u32[]{:S(2)}) %collective-permute-start.1) | collective-permute-done | bytes 131104 | tf_op jit(solution)/shard_map/ppermute | solution.py:227
  19.9 2.4 %collective-permute-done.2 = bf16[2,32,1024]{2,1,0:T(8,128)(2,1)S(1)} collective-permute-done((bf16[2,32,1024]{2,1,0:T(8,128)(2,1)S(1)}, bf16[2,32,1024]{2,1,0:T(8,128)(2,1)S(1)}, u32[]{:S(2)}, u32[]{:S(2)}) %collective-permute-start.2) | collective-permute-done | bytes 131104 | tf_op jit(solution)/shard_map/ppermute | solution.py:227
  22.3 0.0 collective-permute-done.3
  22.4 0.1 collective-permute-start.4
  22.5 0.0 copy-done.4
  22.5 0.1 copy.13.inv.refs_2_
  22.6 0.0 copy-done.3
  22.6 0.1 copy.10
  22.7 0.1 reshape.24.list_ref.refs_1_
  23.4 1.0 %collective-permute-done.4.far.refs_6_ = bf16[8,32,1024]{2,1,0:T(8,128)(2,1)S(1)} collective-permute-done((bf16[8,32,1024]{2,1,0:T(8,128)(2,1)S(1)}, bf16[8,32,1024]{2,1,0:T(8,128)(2,1)S(1)}, u32[]{:S(2)}, u32[]{:S(2)}) %collective-permute-start.4) | collective-permute-done | bytes 524320 | tf_op jit(solution)/shard_map/ppermute | solution.py:227
  24.4 1.5 %prepare_rows.1 = (bf16[6,1024,48]{2,1,0:T(8,128)(2,1)S(1)}, bf16[6,48,1024]{2,1,0:T(8,128)(2,1)S(1)}) custom-call(s32[1]{0:T(128)} %bitcast.27.live_ref, s32[12]{0:T(128)S(1)} %reshape.24.list_ref.refs_1_, f32[32,1]{1,0:T(8,128)S(1)} %copy.13.inv.refs_2_, bf16[8,32,1024]{2,1,0:T(8,128)(2,1)S(1)} %constant_dynamic-update-slice_fusion.near.refs_5_, ...), custom_call_target="tpu_custom_call" | custom-call | flops 2000000000 | bytes 1000000 | tf_op jit(solution)/shard_map/prepare_rows/pallas_call | solution.py:183
  25.9 0.0 copy-start
  25.9 0.8 %copy-done = bf16[6,48,1024]{2,1,0:T(8,128)(2,1)} copy-done((bf16[6,48,1024]{2,1,0:T(8,128)(2,1)}, bf16[6,48,1024]{2,1,0:T(8,128)(2,1)S(1)}, u32[]{:S(2)}) %copy-start) | copy-done | bytes 589848
  26.7 6.5 %all-to-all-done.refs_4_ = bf16[16,48,512]{2,1,0:T(8,128)(2,1)S(1)} async-done(((bf16[16,48,512]{2,1,0:T(8,128)(2,1)}), bf16[16,48,512]{2,1,0:T(8,128)(2,1)S(1)}, u32[]{:S(2)}, u32[]{:S(2)}) %all-to-all-start) | async-done | bytes 786464 | tf_op jit(solution)/shard_map/all_to_all | solution.py:259
  33.2 1.0 %collective-permute-start.5 = (bf16[16,16,512]{2,1,0:T(8,128)(2,1)S(1)}, bf16[16,16,512]{2,1,0:T(8,128)(2,1)S(1)}, u32[]{:S(2)}, u32[]{:S(2)}) collective-permute-start(bf16[16,16,512]{2,1,0:T(8,128)(2,1)S(1)} %slice.47), channel_id=1, source_target_pairs={{0,128},{16,144},{32,160},{48,176},{64,192},{80,208},{96,224},{112... | collective-permute-start | bytes 786440 | tf_op jit(solution)/shard_map/ppermute | solution.py:253
  34.2 0.0 copy-start.1
  34.2 6.9 %first_half.1 = (f32[16,32,1024]{2,1,0:T(8,128)S(1)}, f32[16,16,512]{2,1,0:T(8,128)S(1)}, bf16[16,16,512]{2,1,0:T(8,128)(2,1)S(1)}, bf16[6,1024,1024]{2,1,0:T(8,128)(2,1)S(1)}) custom-call(s32[1]{0:T(128)} %bitcast.28.refs_0_, s32[12]{0:T(128)S(1)} %reshape.24.list_ref.refs_1_, f32[32,1]{1,0:T(8,128)S(1)} %copy.13.inv.refs_2_, ...), custom_call_target="tpu_custom_call" | custom-call | flops 10000000000 | bytes 10000000 | tf_op jit(solution)/shard_map/first_half/pallas_call | solution.py:214
  41.1 0.1 collective-permute-start.6
  41.2 0.0 collective-permute-done.5.refs_6_
  41.2 0.0 copy-done.1
  41.3 6.2 %second_half.1 = (bf16[8,32,1024]{2,1,0:T(8,128)(2,1)S(1)}, bf16[8,32,1024]{2,1,0:T(8,128)(2,1)S(1)}, bf16[16,48,512]{2,1,0:T(8,128)(2,1)}) custom-call(s32[1]{0:T(128)} %bitcast.29.refs_0_, s32[12]{0:T(128)S(1)} %reshape.24.list_ref.refs_1_, f32[32,1]{1,0:T(8,128)S(1)} %copy.13.inv.refs_2_, bf16[6,1024,48]{2,1,0:T(8,128)(2,1)S(1)} %get-tuple-element.14.refs_3_, ...), custom_call_target="tpu_custom_call" | custom-call | flops 10000000000 | bytes 10000000 | tf_op jit(solution)/shard_map/second_half/pallas_call | solution.py:214
  47.5 0.0 collective-permute-start.7
  47.5 0.1 collective-permute-done.6
  47.6 0.8 fusion
  48.4 9.1 %all-to-all-start.1 = ((bf16[16,48,512]{2,1,0:T(8,128)(2,1)}), bf16[16,48,512]{2,1,0:T(8,128)(2,1)S(1)}, u32[]{:S(2)}, u32[]{:S(2)}) async-start(bf16[16,48,512]{2,1,0:T(8,128)(2,1)} %fusion), calls=%async_computation.1 | async-start | bytes 1572864 | tf_op jit(solution)/shard_map/all_to_all | solution.py:263
  57.5 0.0 collective-permute-done.7
  57.5 0.2 add_convert_fusion
  57.7 0.9 %collective-permute-start.10 = (bf16[2,32,1024]{2,1,0:T(8,128)(2,1)S(1)}, bf16[2,32,1024]{2,1,0:T(8,128)(2,1)S(1)}, u32[]{:S(2)}, u32[]{:S(2)}) collective-permute-start(bf16[2,32,1024]{2,1,0:T(8,128)(2,1)S(1)} %get-tuple-element.24), channel_id=1, source_target_pairs={{0,4},{1,5},{2,6},{3,7},{4,8},{5,9},{6,10},{7,11},{8,12},{9,13},{1... | collective-permute-start | bytes 393224 | tf_op jit(solution)/shard_map/ppermute | solution.py:227
  58.7 2.4 %collective-permute-start.8 = (bf16[2,32,1024]{2,1,0:T(8,128)(2,1)S(1)}, bf16[2,32,1024]{2,1,0:T(8,128)(2,1)S(1)}, u32[]{:S(2)}, u32[]{:S(2)}) collective-permute-start(bf16[2,32,1024]{2,1,0:T(8,128)(2,1)S(1)} %get-tuple-element.23), channel_id=1, source_target_pairs={{0,12},{1,13},{2,14},{3,15},{4,0},{5,1},{6,2},{7,3},{8,4},{9,5},{1... | collective-permute-start | bytes 393224 | tf_op jit(solution)/shard_map/ppermute | solution.py:227
  61.0 1.8 %collective-permute-start.9 = (bf16[2,32,1024]{2,1,0:T(8,128)(2,1)S(1)}, bf16[2,32,1024]{2,1,0:T(8,128)(2,1)S(1)}, u32[]{:S(2)}, u32[]{:S(2)}) collective-permute-start(bf16[2,32,1024]{2,1,0:T(8,128)(2,1)S(1)} %get-tuple-element.25), channel_id=1, source_target_pairs={{0,8},{1,9},{2,10},{3,11},{4,12},{5,13},{6,14},{7,15},{8,0},{9,1},... | collective-permute-start | bytes 393224 | tf_op jit(solution)/shard_map/ppermute | solution.py:227
  62.9 1.8 %collective-permute-done.10 = bf16[2,32,1024]{2,1,0:T(8,128)(2,1)S(1)} collective-permute-done((bf16[2,32,1024]{2,1,0:T(8,128)(2,1)S(1)}, bf16[2,32,1024]{2,1,0:T(8,128)(2,1)S(1)}, u32[]{:S(2)}, u32[]{:S(2)}) %collective-permute-start.10) | collective-permute-done | bytes 131104 | tf_op jit(solution)/shard_map/ppermute | solution.py:227
  64.7 2.1 %collective-permute-done.8 = bf16[2,32,1024]{2,1,0:T(8,128)(2,1)S(1)} collective-permute-done((bf16[2,32,1024]{2,1,0:T(8,128)(2,1)S(1)}, bf16[2,32,1024]{2,1,0:T(8,128)(2,1)S(1)}, u32[]{:S(2)}, u32[]{:S(2)}) %collective-permute-start.8) | collective-permute-done | bytes 131104 | tf_op jit(solution)/shard_map/ppermute | solution.py:227
  66.8 1.3 %collective-permute-done.9 = bf16[2,32,1024]{2,1,0:T(8,128)(2,1)S(1)} collective-permute-done((bf16[2,32,1024]{2,1,0:T(8,128)(2,1)S(1)}, bf16[2,32,1024]{2,1,0:T(8,128)(2,1)S(1)}, u32[]{:S(2)}, u32[]{:S(2)}) %collective-permute-start.9) | collective-permute-done | bytes 131104 | tf_op jit(solution)/shard_map/ppermute | solution.py:227
  68.1 0.1 convert_add_fusion
  68.2 1.7 %collective-permute-start.11 = (bf16[32,1024]{1,0:T(8,128)(2,1)S(1)}, bf16[32,1024]{1,0:T(8,128)(2,1)S(1)}, u32[]{:S(2)}, u32[]{:S(2)}) collective-permute-start(bf16[32,1024]{1,0:T(8,128)(2,1)S(1)} %fusion.5), channel_id=1, source_target_pairs={{0,2},{1,3},{2,0},{3,1},{4,6},{5,7},{6,4},{7,5},{8,10},{9,11},{10,... | collective-permute-start | bytes 196616 | tf_op jit(solution)/shard_map/ppermute | solution.py:227
  69.9 10.0 %all-to-all-done.1 = bf16[16,48,512]{2,1,0:T(8,128)(2,1)S(1)} async-done(((bf16[16,48,512]{2,1,0:T(8,128)(2,1)}), bf16[16,48,512]{2,1,0:T(8,128)(2,1)S(1)}, u32[]{:S(2)}, u32[]{:S(2)}) %all-to-all-start.1) | async-done | bytes 786464 | tf_op jit(solution)/shard_map/all_to_all | solution.py:263
  79.9 0.2 convert_element_type.39
  80.1 0.1 slice_reduce_fusion
  80.2 0.0 collective-permute-done.11
  80.2 0.7 fusion.4
  (13 shorter events, 0.2 us)
Async XLA Ops:
  0.0 12.5 %collective-permute-start = (bf16[32,1024]{1,0:T(8,128)(2,1)}, bf16[32,1024]{1,0:T(8,128)(2,1)S(1)}, u32[]{:S(2)}, u32[]{:S(2)}) collective-permute-start(bf16[32,1024]{1,0:T(8,128)(2,1)} %bitcast.31), channel_id=1, source_target_pairs={{0,2},{1,3},{2,0},{3,1},{4,6},{5,7},{6,4},{7,5},{8,10},{9,11},{10,... | collective-permute-start | bytes 196616 | tf_op jit(solution)/shard_map/ppermute | solution.py:227
  2.9 9.6 %copy-start.2 = (bf16[1,1,32,1024]{3,2,1,0:T(8,128)(2,1)S(1)}, bf16[1,1,32,1024]{3,2,1,0:T(8,128)(2,1)}, u32[]{:S(2)}) copy-start(bf16[1,1,32,1024]{3,2,1,0:T(8,128)(2,1)} %param.5) | copy-start | bytes 196612
  3.9 18.6 %copy-start.4 = (f32[32]{0:T(128)S(1)}, f32[32]{0:T(128)}, u32[]{:S(2)}) copy-start(f32[32]{0:T(128)} %param.6) | copy-start | bytes 388
  3.9 18.7 %copy-start.3 = (s32[1,1,6,2]{2,3,1,0:T(2,128)S(1)}, s32[1,1,6,2]{2,3,1,0:T(2,128)}, u32[]{:S(2)}) copy-start(s32[1,1,6,2]{2,3,1,0:T(2,128)} %param.8) | copy-start | bytes 148
  3.9 29.3 %all-to-all-start = ((bf16[16,48,512]{2,1,0:T(8,128)(2,1)}), bf16[16,48,512]{2,1,0:T(8,128)(2,1)S(1)}, u32[]{:S(2)}, u32[]{:S(2)}) async-start(bf16[16,48,512]{2,1,0:T(8,128)(2,1)} %pad_maximum_fusion), calls=%async_computation | async-start | bytes 1572864 | tf_op jit(solution)/shard_map/all_to_all | solution.py:259
  12.6 7.3 %collective-permute-start.1 = (bf16[2,32,1024]{2,1,0:T(8,128)(2,1)S(1)}, bf16[2,32,1024]{2,1,0:T(8,128)(2,1)S(1)}, u32[]{:S(2)}, u32[]{:S(2)}) collective-permute-start(bf16[2,32,1024]{2,1,0:T(8,128)(2,1)S(1)} %pad_maximum_fusion.1), channel_id=1, source_target_pairs={{0,4},{1,5},{2,6},{3,7},{4,8},{5,9},{6,10},{7,11},{8,12},{9,13},{1... | collective-permute-start | bytes 393224 | tf_op jit(solution)/shard_map/ppermute | solution.py:227
  14.1 8.2 %collective-permute-start.2 = (bf16[2,32,1024]{2,1,0:T(8,128)(2,1)S(1)}, bf16[2,32,1024]{2,1,0:T(8,128)(2,1)S(1)}, u32[]{:S(2)}, u32[]{:S(2)}) collective-permute-start(bf16[2,32,1024]{2,1,0:T(8,128)(2,1)S(1)} %pad_maximum_fusion.1), channel_id=1, source_target_pairs={{0,8},{1,9},{2,10},{3,11},{4,12},{5,13},{6,14},{7,15},{8,0},{9,1},... | collective-permute-start | bytes 393224 | tf_op jit(solution)/shard_map/ppermute | solution.py:227
  16.9 5.5 %collective-permute-start.3 = (bf16[2,32,1024]{2,1,0:T(8,128)(2,1)S(1)}, bf16[2,32,1024]{2,1,0:T(8,128)(2,1)S(1)}, u32[]{:S(2)}, u32[]{:S(2)}) collective-permute-start(bf16[2,32,1024]{2,1,0:T(8,128)(2,1)S(1)} %pad_maximum_fusion.1), channel_id=1, source_target_pairs={{0,12},{1,13},{2,14},{3,15},{4,0},{5,1},{6,2},{7,3},{8,4},{9,5},{1... | collective-permute-start | bytes 393224 | tf_op jit(solution)/shard_map/ppermute | solution.py:227
  22.4 2.0 %collective-permute-start.4 = (bf16[8,32,1024]{2,1,0:T(8,128)(2,1)S(1)}, bf16[8,32,1024]{2,1,0:T(8,128)(2,1)S(1)}, u32[]{:S(2)}, u32[]{:S(2)}) collective-permute-start(bf16[8,32,1024]{2,1,0:T(8,128)(2,1)S(1)} %constant_dynamic-update-slice_fusion.near.refs_5_), channel_id=1, source_target_pairs={{0,1},{1,0},{2,3},{3,2},{4,5},{5,4},{6,7},{7,6},{8,9},{9,8},{10,11... | collective-permute-start | bytes 1572872 | tf_op jit(solution)/shard_map/ppermute | solution.py:227
  25.9 0.8 %copy-start = (bf16[6,48,1024]{2,1,0:T(8,128)(2,1)}, bf16[6,48,1024]{2,1,0:T(8,128)(2,1)S(1)}, u32[]{:S(2)}) copy-start(bf16[6,48,1024]{2,1,0:T(8,128)(2,1)S(1)} %get-tuple-element.15.refs_5_) | copy-start | bytes 1769476
  33.2 8.0 %collective-permute-start.5 = (bf16[16,16,512]{2,1,0:T(8,128)(2,1)S(1)}, bf16[16,16,512]{2,1,0:T(8,128)(2,1)S(1)}, u32[]{:S(2)}, u32[]{:S(2)}) collective-permute-start(bf16[16,16,512]{2,1,0:T(8,128)(2,1)S(1)} %slice.47), channel_id=1, source_target_pairs={{0,128},{16,144},{32,160},{48,176},{64,192},{80,208},{96,224},{112... | collective-permute-start | bytes 786440 | tf_op jit(solution)/shard_map/ppermute | solution.py:253
  34.2 7.0 %copy-start.1 = (bf16[6,48,1024]{2,1,0:T(8,128)(2,1)S(1)}, bf16[6,48,1024]{2,1,0:T(8,128)(2,1)}, u32[]{:S(2)}) copy-start(bf16[6,48,1024]{2,1,0:T(8,128)(2,1)} %copy-done) | copy-start | bytes 1769476
  41.1 6.5 %collective-permute-start.6 = (bf16[16,16,512]{2,1,0:T(8,128)(2,1)S(1)}, bf16[16,16,512]{2,1,0:T(8,128)(2,1)S(1)}, u32[]{:S(2)}, u32[]{:S(2)}) collective-permute-start(bf16[16,16,512]{2,1,0:T(8,128)(2,1)S(1)} %get-tuple-element.20), channel_id=1, source_target_pairs={{0,128},{16,144},{32,160},{48,176},{64,192},{80,208},{96,224},{112... | collective-permute-start | bytes 786440 | tf_op jit(solution)/shard_map/ppermute | solution.py:253
  47.5 10.0 %collective-permute-start.7 = (bf16[8,32,1024]{2,1,0:T(8,128)(2,1)S(1)}, bf16[8,32,1024]{2,1,0:T(8,128)(2,1)S(1)}, u32[]{:S(2)}, u32[]{:S(2)}) collective-permute-start(bf16[8,32,1024]{2,1,0:T(8,128)(2,1)S(1)} %get-tuple-element.22), channel_id=1, source_target_pairs={{0,1},{1,0},{2,3},{3,2},{4,5},{5,4},{6,7},{7,6},{8,9},{9,8},{10,11... | collective-permute-start | bytes 1572872 | tf_op jit(solution)/shard_map/ppermute | solution.py:227
  48.4 31.5 %all-to-all-start.1 = ((bf16[16,48,512]{2,1,0:T(8,128)(2,1)}), bf16[16,48,512]{2,1,0:T(8,128)(2,1)S(1)}, u32[]{:S(2)}, u32[]{:S(2)}) async-start(bf16[16,48,512]{2,1,0:T(8,128)(2,1)} %fusion), calls=%async_computation.1 | async-start | bytes 1572864 | tf_op jit(solution)/shard_map/all_to_all | solution.py:263
  57.7 6.9 %collective-permute-start.10 = (bf16[2,32,1024]{2,1,0:T(8,128)(2,1)S(1)}, bf16[2,32,1024]{2,1,0:T(8,128)(2,1)S(1)}, u32[]{:S(2)}, u32[]{:S(2)}) collective-permute-start(bf16[2,32,1024]{2,1,0:T(8,128)(2,1)S(1)} %get-tuple-element.24), channel_id=1, source_target_pairs={{0,4},{1,5},{2,6},{3,7},{4,8},{5,9},{6,10},{7,11},{8,12},{9,13},{1... | collective-permute-start | bytes 393224 | tf_op jit(solution)/shard_map/ppermute | solution.py:227
  58.7 8.1 %collective-permute-start.8 = (bf16[2,32,1024]{2,1,0:T(8,128)(2,1)S(1)}, bf16[2,32,1024]{2,1,0:T(8,128)(2,1)S(1)}, u32[]{:S(2)}, u32[]{:S(2)}) collective-permute-start(bf16[2,32,1024]{2,1,0:T(8,128)(2,1)S(1)} %get-tuple-element.23), channel_id=1, source_target_pairs={{0,12},{1,13},{2,14},{3,15},{4,0},{5,1},{6,2},{7,3},{8,4},{9,5},{1... | collective-permute-start | bytes 393224 | tf_op jit(solution)/shard_map/ppermute | solution.py:227
  61.0 7.0 %collective-permute-start.9 = (bf16[2,32,1024]{2,1,0:T(8,128)(2,1)S(1)}, bf16[2,32,1024]{2,1,0:T(8,128)(2,1)S(1)}, u32[]{:S(2)}, u32[]{:S(2)}) collective-permute-start(bf16[2,32,1024]{2,1,0:T(8,128)(2,1)S(1)} %get-tuple-element.25), channel_id=1, source_target_pairs={{0,8},{1,9},{2,10},{3,11},{4,12},{5,13},{6,14},{7,15},{8,0},{9,1},... | collective-permute-start | bytes 393224 | tf_op jit(solution)/shard_map/ppermute | solution.py:227
  68.2 12.0 %collective-permute-start.11 = (bf16[32,1024]{1,0:T(8,128)(2,1)S(1)}, bf16[32,1024]{1,0:T(8,128)(2,1)S(1)}, u32[]{:S(2)}, u32[]{:S(2)}) collective-permute-start(bf16[32,1024]{1,0:T(8,128)(2,1)S(1)} %fusion.5), channel_id=1, source_target_pairs={{0,2},{1,3},{2,0},{3,1},{4,6},{5,7},{6,4},{7,5},{8,10},{9,11},{10,... | collective-permute-start | bytes 196616 | tf_op jit(solution)/shard_map/ppermute | solution.py:227
